TPU v7x, 128 devices: a whole 4x4x4 slice. The times are simulated.
128 devices in a mesh: seq: 16 (over x_hi, y, core), blk: 8 (over x_lo, z).
Axes of the slice: x: 4 (x_hi: 2, x_lo: 2; x = x_hi * 2 + x_lo), y: 4, z: 4, core: 2. Of those that a mesh axis runs over, the one named last changes fastest.
Arguments:
- tokens: bfloat16 [16384, 1536], P(('seq', 'blk')), may hold values from -6 to 6
- boundary: int32 [16384], P(('seq', 'blk')), may hold values from 0 to 1, as said below
- heads_in: bfloat16 [1536, 3, 1536], P(None, None, 'blk')
- heads_out: bfloat16 [1536, 1536], P('blk'), may hold values from -0.15625 to 0.15625
- gate_up: bfloat16 [1536, 2, 4096], P(None, None, 'blk'), may hold values from -0.15625 to 0.15625
- down_weight: bfloat16 [4096, 1536], P('blk'), may hold values from -0.09375 to 0.09375
- widen: bfloat16 [1536, 4096], P(None, 'blk'), may hold values from -0.15625 to 0.15625
- heads_in_two: bfloat16 [4096, 3, 4096], P(None, None, 'blk')
- heads_out_two: bfloat16 [4096, 4096], P('blk'), may hold values from -0.09375 to 0.09375
Outputs:
- level_one: bfloat16 [16384, 1536], P(('seq', 'blk'))
- level_two: bfloat16 [8192, 4096], P('seq', 'blk')
Inputs may be any that keep to these rules, and one draw needn't show every extreme that they name: `boundary`: each aligned block of 1024 consecutive rows holds between 256 and 512 ones, and some block holds exactly 512.
All inputs are finite; a program needn't handle non-finite values.
Results may differ from a plain program's by a relative error of at most 0.04.
Values may be sent and summed in bfloat16 or wider, within the bound.
No kernel may reach another device: no remote copies, remote signals or barrier semaphores. Data moves between devices by JAX's collectives and lax.ppermute only.
A program may use at most 128 MiB of HBM per device.

v0:
```python
import jax
import jax.numpy as jnp
from jax import lax
from jax.experimental import pallas as pl
from jax.experimental.pallas import tpu as pltpu
from jax.sharding import PartitionSpec as P

D1 = 1536
H1 = 24
D2 = 4096
H2 = 32
WIN = 512
EXT = 16
SENT = 128
BF16 = jnp.bfloat16
F32 = jnp.float32
MASKED = -1e30
SCORE_FACTOR = 128 ** (-0.5) * 1.4426950408889634

PLACES = ((0, 0), (1, 0), (0, 1), (0, 3), (0, 2), (1, 2), (1, 1), (1, 3))


def flip_x(value):
    return lax.ppermute(value, "blk", [(i, i ^ 4) for i in range(8)])


def turn_z(value, steps):
    return lax.ppermute(value, "blk", [(i, (i & 4) | ((i + steps) & 3)) for i in range(8)])


def later(array, value):
    return array + (value[0, 0].astype(F32) * 0.0).astype(array.dtype)


def gather_blk(own, between=None):
    across = flip_x(own)
    behind = turn_z(own, 1)
    ahead = turn_z(own, 3)
    first = jnp.concatenate([own, across], axis=0)
    second = jnp.concatenate([ahead, behind], axis=0)
    if between is not None:
        first, second = later(first, between), later(second, between)
    opposite = turn_z(first, 2)
    diagonal = flip_x(second)
    near = jnp.concatenate([first, second], axis=0)
    return near, opposite, diagonal


def reduce_first(far):
    count = far.shape[0] // 4
    return turn_z(far[: 2 * count], 2), flip_x(far[2 * count :])


def reduce_second(near, opposite, diagonal):
    count = near.shape[0] // 4

    def plus(block, other):
        return near[block * count : (block + 1) * count].astype(F32) + other.astype(F32)

    across = flip_x(plus(1, opposite[count:]).astype(BF16))
    behind = turn_z(plus(2, diagonal[:count]).astype(BF16), 1)
    ahead = turn_z(plus(3, diagonal[count:]).astype(BF16), 3)
    return (
        plus(0, opposite[:count])
        + across.astype(F32)
        + behind.astype(F32)
        + ahead.astype(F32)
    )


def reduce_blk(near, far):
    return reduce_second(near, *reduce_first(far))


def normalize(values):
    floats = values.astype(F32)
    return floats * lax.rsqrt(jnp.mean(floats * floats, axis=-1, keepdims=True) + 1e-06)


def dot(left, right):
    return jnp.dot(left, right, preferred_element_type=F32)


def dot_t(left, right):
    return lax.dot_general(left, right, (((1,), (1,)), ((), ())), preferred_element_type=F32)


def window_kernel(blocks, info, qkv, halo, before, out):
    rows, width, size, stride = 128, D1 // 8, D1 // H1, SENT
    key_count = WIN + rows
    i = lax.broadcasted_iota(jnp.int32, (key_count, rows), 1)
    j = lax.broadcasted_iota(jnp.int32, (key_count, rows), 0)
    band = (j > i) & (j <= i + WIN)
    seq_position = info[8]
    if before is not None:
        out[...] = before[...]
    for n in blocks:
        place = info[n]
        keys, values = [], []
        for k in range(n - 4, n + 1):
            if k >= 0:
                start = pl.multiple_of(info[k] * stride, 16)
                block = qkv[pl.ds(start, rows), :]
                keys.append(block[:, :width])
                values.append(block[:, width : 2 * width])
            else:
                block = halo[(k + 4) * rows : (k + 5) * rows, :]
                keys.append(block[:, :width])
                values.append(block[:, width:])
        keys = jnp.concatenate(keys, axis=0)
        values = jnp.concatenate(values, axis=0)
        queries = qkv[pl.ds(pl.multiple_of(place * stride, 16), rows), 2 * width :]
        allowed = band
        if n < 4:
            allowed = band & (j + ((n - 4) * rows + seq_position * 1024) >= 0)
        values = values.T
        parts = []
        for h in range(width // size):
            cut = slice(h * size, (h + 1) * size)
            scores = dot_t(keys[:, cut], queries[:, cut]) * size ** (-0.5)
            scores = jnp.where(allowed, scores, MASKED)
            largest = jnp.max(scores, axis=0, keepdims=True)
            weights = jnp.exp(scores - largest)
            total = jnp.sum(weights, axis=0, keepdims=True)
            parts.append(dot(values[cut, :], weights.astype(BF16)) / total)
        out[pl.ds(pl.multiple_of(place * rows, 16), rows), :] = jnp.concatenate(
            parts, axis=0
        ).T.astype(BF16)


def window_attend(info, qkv, halo=None, before=None):
    if halo is None:
        def kernel(info, qkv, out):
            window_kernel(range(4, 8), info, qkv, None, None, out)

        operands = (info, qkv)
    else:
        def kernel(info, qkv, halo, before, out):
            window_kernel(range(4), info, qkv, halo, before, out)

        operands = (info, qkv, halo, before)
    vmem = pl.BlockSpec(memory_space=pltpu.VMEM)
    return pl.pallas_call(
        kernel,
        out_shape=jax.ShapeDtypeStruct((1024, D1 // 8), BF16),
        in_specs=[pl.BlockSpec(memory_space=pltpu.SMEM)] + [vmem] * (len(operands) - 1),
        out_specs=vmem,
        compiler_params=pltpu.CompilerParams(vmem_limit_bytes=32 * 2**20),
        cost_estimate=pl.CostEstimate(
            flops=12 * 128 * 640 * 256, bytes_accessed=2 * 2**20, transcendentals=12 * 128 * 640
        ),
        name="window_late" if halo is None else "window_early",
    )(*operands)


def prepare_kernel(tokens, out):
    floats = tokens[...].astype(F32)
    scale = lax.rsqrt(jnp.mean(floats * floats, axis=-1, keepdims=True) + 1e-06)
    out[...] = (floats * scale).astype(BF16)


def prepare(tokens):
    return pl.pallas_call(
        prepare_kernel,
        out_shape=jax.ShapeDtypeStruct(tokens.shape, BF16),
        in_specs=[pl.BlockSpec(memory_space=pltpu.VMEM)],
        out_specs=pl.BlockSpec(memory_space=pltpu.VMEM),
        name="prepare",
    )(tokens)


def near_kernel(rows, weights, out):
    out[:, :384] = dot_t(rows[...], weights[192:, :]).astype(BF16)
    out[:, 384:] = dot_t(rows[...], weights[:192, :]).astype(BF16)


def far_kernel(info, near, opposite, diagonal, weights, out, edge):
    half = 4 * SENT
    out[:half, :] = near[...]
    cuts = ((slice(half, half + 2 * SENT), opposite), (slice(half + 2 * SENT, 2 * half), diagonal))
    for cut, rows in cuts:
        out[cut, :384] = dot_t(rows[...], weights[192:, :]).astype(BF16)
    for k in range(4):
        start = pl.multiple_of(info[4 + k] * SENT, 16)
        edge[k * 128 : (k + 1) * 128, :] = out[pl.ds(start, 128), :384]
    for cut, rows in cuts:
        out[cut, 384:] = dot_t(rows[...], weights[:192, :]).astype(BF16)


def project_one(weights, near, info=None, opposite=None, diagonal=None):
    vmem = pl.BlockSpec(memory_space=pltpu.VMEM)
    cost = pl.CostEstimate(flops=2 * 576 * 576 * D1, bytes_accessed=5 * 2**20, transcendentals=0)
    params = pltpu.CompilerParams(vmem_limit_bytes=24 * 2**20)
    if info is None:
        return pl.pallas_call(
            near_kernel,
            out_shape=jax.ShapeDtypeStruct((4 * SENT, 576), BF16),
            in_specs=[vmem] * 2,
            out_specs=vmem,
            compiler_params=params,
            cost_estimate=cost,
            name="project_near",
        )(near, weights)
    return pl.pallas_call(
        far_kernel,
        out_shape=(
            jax.ShapeDtypeStruct((8 * SENT, 576), BF16), jax.ShapeDtypeStruct((WIN, 384), BF16)
        ),
        in_specs=[pl.BlockSpec(memory_space=pltpu.SMEM)] + [vmem] * 4,
        out_specs=(vmem, vmem),
        compiler_params=params,
        cost_estimate=cost,
        name="project_far",
    )(info, near, opposite, diagonal, weights)


def pieces_kernel(near, opposite, diagonal, _, out, marks):
    blocks = [(part, k * 208) for part, n in ((near, 4), (opposite, 2), (diagonal, 2)) for k in range(n)]
    rows = []
    for k, (part, start) in enumerate(blocks):
        out[k * 192 : (k + 1) * 192, :] = part[start : start + 192, :]
        rows.append(part[start + 192 : start + 208, :128].astype(F32)[:1])
    marks[...] = jnp.concatenate(rows, axis=0)


def collect_pieces(near, opposite, diagonal, before):
    vmem = pl.BlockSpec(memory_space=pltpu.VMEM)
    return pl.pallas_call(
        pieces_kernel,
        out_shape=(
            jax.ShapeDtypeStruct((1536, 512), BF16), jax.ShapeDtypeStruct((8, 128), F32)
        ),
        in_specs=[vmem] * 3 + [pl.BlockSpec(memory_space=pl.ANY)],
        out_specs=(vmem, vmem),
        compiler_params=pltpu.CompilerParams(vmem_limit_bytes=16 * 2**20),
        name="collect_pieces",
    )(near, opposite, diagonal, before)


def mlp_kernel(gate, up, down, *refs):
    out, first = refs[-1], 0
    for rows in refs[:-1]:
        def some(step, _, rows=rows, first=first):
            start = pl.multiple_of(step * 256, 256)
            block = rows[pl.ds(start, 256), :]
            gated = dot(block, gate[...])
            hidden = gated / (1.0 + jnp.exp(-gated)) * dot(block, up[...])
            out[pl.ds(first + start, 256), :] = dot(hidden.astype(BF16), down[...]).astype(BF16)
            return 0

        lax.fori_loop(0, rows.shape[0] // 256, some, 0)
        first += rows.shape[0]


def mlp(gate, up, down, *rows):
    return pl.pallas_call(
        mlp_kernel,
        out_shape=jax.ShapeDtypeStruct((512, D1), BF16),
        in_specs=[pl.BlockSpec(memory_space=pltpu.VMEM)] * (3 + len(rows)),
        out_specs=pl.BlockSpec(memory_space=pltpu.VMEM),
        compiler_params=pltpu.CompilerParams(vmem_limit_bytes=32 * 2**20),
        cost_estimate=pl.CostEstimate(
            flops=2 * 512 * 1536 * 1536, bytes_accessed=8 * 2**20, transcendentals=512 * 512
        ),
        name="mlp",
    )(gate, up, down, *rows)


def project_kernel(
    info, near, opposite, diagonal, pieces, weights, valid, chunks, wide_own, pooled, total, squares
):
    step = pl.program_id(0)
    y = info[8]

    @pl.when(step == 0)
    def _():
        pooled[:256, :] = near[...]
        pooled[256:384, :] = opposite[...]
        pooled[384:, :] = diagonal[...]
        total[...] = jnp.zeros_like(total)
        squares[...] = jnp.zeros_like(squares)

    wide = dot(pooled[...], pieces[...].reshape(D1, 512)).astype(BF16)
    floats = wide.astype(F32)
    squares[...] += jnp.broadcast_to(
        jnp.sum(floats * floats, axis=-1, keepdims=True), squares.shape
    )
    for i in range(3):
        total[:, i * 512 : (i + 1) * 512] += dot(wide, weights[i])

    @pl.when(step == 0)
    def _():
        for p in range(8):
            start = pl.multiple_of(info[p] * 64, 64)
            wide_own[pl.ds(start, 64), :] = wide[p * 64 : (p + 1) * 64]

    @pl.when(step == 7)
    def _():
        scale = lax.rsqrt(squares[...] / D2 + 1e-06)
        for k in range(4):
            head = (y + k) & 3
            for i in range(3):
                cut = slice(i * 128, (i + 1) * 128)
                lanes = pl.ds(pl.multiple_of(i * 512 + head * 128, 128), 128)
                part = total[:, lanes] * (scale * SCORE_FACTOR if i == 0 else scale)
                part = part.astype(BF16)
                for p in range(8):
                    start = pl.multiple_of(info[p] * 64, 64)
                    chunks[k, pl.ds(start, 64), cut] = part[p * 64 : (p + 1) * 64]
                chunks[k, 512:, cut] = valid[...]


def project_two(info, pooled, pieces, weights, valid):
    return pl.pallas_call(
        project_kernel,
        out_shape=(
            jax.ShapeDtypeStruct((4, 512 + EXT, 384), BF16),
            jax.ShapeDtypeStruct((512, 512), BF16),
        ),
        grid_spec=pltpu.PrefetchScalarGridSpec(
            num_scalar_prefetch=1,
            grid=(8,),
            in_specs=[
                *[pl.BlockSpec((k, D1), lambda s, info: (0, 0)) for k in (256, 128, 128)],
                pl.BlockSpec((8, 1, 192, 512), lambda s, info: (0, s, 0, 0)),
                pl.BlockSpec((3, 512, 512), lambda s, info: (0, info[s], 0)),
                pl.BlockSpec((EXT, 128), lambda s, info: (0, 0)),
            ],
            out_specs=(
                pl.BlockSpec((4, 512 + EXT, 384), lambda s, info: (0, 0, 0)),
                pl.BlockSpec((512, 512), lambda s, info: (0, 0)),
            ),
            scratch_shapes=[
                pltpu.VMEM((512, D1), BF16),
                pltpu.VMEM((512, 1536), F32),
                pltpu.VMEM((512, 128), F32),
            ],
        ),
        compiler_params=pltpu.CompilerParams(vmem_limit_bytes=40 * 2**20),
        cost_estimate=pl.CostEstimate(
            flops=4 * 512 * 4096 * 1536, bytes_accessed=28 * 2**20, transcendentals=512
        ),
        name="project_two",
    )(info, *pooled, pieces, weights, valid)


def causal_kernel(own_part, info, queries, kv_pair, start, start_stats, out, out_stats, keys, values, even, odd):
    half, core, y = info[0], info[1], info[2]
    slot = pl.program_id(0)
    own_pair = (y + slot) & 3

    @pl.when(slot == 0)
    def _():
        def prepare(block, _):
            row = lax.broadcasted_iota(jnp.int32, (512, 128), 0).astype(F32)
            lane = lax.broadcasted_iota(jnp.int32, (512, 128), 1)
            for which, kv in enumerate(kv_pair):
                count = jnp.sum(kv[block, 512 : 512 + EXT, :128].astype(F32))
                invalid = (lane == 0) & (row >= count)
                keys[which * 4 + block, :, :128] = kv[block, :512, :128]
                keys[which * 4 + block, :, 128:] = jnp.where(invalid, MASKED, 0.0).astype(BF16)
                values[which * 4 + block] = kv[block, :512, 128:].T
            return 0

        lax.fori_loop(0, 4, prepare, 0)

    lane = lax.broadcasted_iota(jnp.int32, (512, 128), 1)
    query = jnp.concatenate([queries[0], jnp.where(lane == 0, 1.0, 0.0).astype(BF16)], axis=1)

    def block_of(pair, which):
        return (which ^ core) * 4 + ((pair - y) & 3)

    def scores_of(pair, which):
        return lax.dot_general(
            keys[block_of(pair, which)], query, (((1,), (1,)), ((), ())), preferred_element_type=F32
        )

    def absorb(scores, pair, which, carry, edge):
        largest, total, sums = carry
        if edge:
            key = lax.broadcasted_iota(jnp.int32, scores.shape, 0) + which * 512
            own = lax.broadcasted_iota(jnp.int32, scores.shape, 1) + core * 512
            scores = jnp.where(key <= own, scores, MASKED)
        new_largest = jnp.maximum(largest, jnp.max(scores, axis=0, keepdims=True))
        decay = jnp.exp2(largest - new_largest)
        weights = jnp.exp2(scores - new_largest)
        total = total * decay + jnp.sum(weights, axis=0, keepdims=True)
        sums = sums * decay + dot(values[block_of(pair, which)], weights.astype(BF16))
        return new_largest, total, sums

    even[...] = scores_of(0, 0)

    def both(pair, carry, edge=False):
        odd[...] = scores_of(pair, 1)
        carry = absorb(even[...], pair, 0, carry, edge)
        if not edge:
            even[...] = scores_of((pair + 1) & 3, 0)
        return absorb(odd[...], pair, 1, carry, edge)

    if own_part:
        carry = (
            jnp.full((1, 512), MASKED, F32), jnp.zeros((1, 512), F32), jnp.zeros((128, 512), F32)
        )
        carry = lax.fori_loop(0, own_pair, both, carry)
        largest, total, sums = both(own_pair, carry, True)
        out[0] = sums
        out_stats[0] = jnp.concatenate([largest, total, jnp.zeros((6, 512), F32)], axis=0)
    else:
        carry = (start_stats[0, 0:1], start_stats[0, 1:2], start[0])
        _, total, sums = lax.fori_loop(0, half * 4, both, carry)
        out[0] = (sums / total).T.astype(BF16)


def causal_attend(own_part, info, queries, kv_pair, start=None):
    def by_slot(*shape):
        return pl.BlockSpec((1, *shape), lambda s, info: (s, 0, 0))

    sums_shape = jax.ShapeDtypeStruct((4, 128, 512), F32)
    stats_shape = jax.ShapeDtypeStruct((4, 8, 512), F32)
    whole = pl.BlockSpec((4, 512 + EXT, 256), lambda s, info: (0, 0, 0))
    in_specs = [by_slot(512, 128), whole, whole]
    operands = [queries, *kv_pair]
    if own_part:
        def kernel(info, queries, kv, other, out, out_stats, *scratch):
            causal_kernel(True, info, queries, (kv, other), None, None, out, out_stats, *scratch)

        out_shape = (sums_shape, stats_shape)
        out_specs = (by_slot(128, 512), by_slot(8, 512))
        tiles = 18
    else:
        def kernel(info, queries, kv, other, start, start_stats, out, *scratch):
            causal_kernel(False, info, queries, (kv, other), start, start_stats, out, None, *scratch)

        out_shape = jax.ShapeDtypeStruct((4, 512, 128), BF16)
        out_specs = by_slot(512, 128)
        in_specs += [by_slot(128, 512), by_slot(8, 512)]
        operands += list(start)
        tiles = 32
    return pl.pallas_call(
        kernel,
        out_shape=out_shape,
        grid_spec=pltpu.PrefetchScalarGridSpec(
            num_scalar_prefetch=1,
            grid=(4,),
            in_specs=in_specs,
            out_specs=out_specs,
            scratch_shapes=[
                pltpu.VMEM((8, 512, 256), BF16),
                pltpu.VMEM((8, 128, 512), BF16),
                pltpu.VMEM((512, 512), F32),
                pltpu.VMEM((512, 512), F32),
            ],
        ),
        compiler_params=pltpu.CompilerParams(vmem_limit_bytes=40 * 2**20),
        cost_estimate=pl.CostEstimate(
            flops=tiles * 512 * 512 * 512, bytes_accessed=4 * 2**20, transcendentals=tiles * 2**18
        ),
        name="causal_own" if own_part else "causal_first_half",
    )(info, *operands)


def turn_y(value, steps, first=0):
    return lax.ppermute(
        value, "seq", [(i, (i & 9) | ((i + 2 * steps) & 6)) for i in range(first, 16)]
    )


def output_kernel(count, info, own, ahead, opposite, behind, weights, out, mixed):
    @pl.when(pl.program_id(0) == 0)
    def _():
        for k, part in enumerate((own, ahead, opposite, behind)):
            head = (info[count] + k) & 3
            mixed[:, pl.ds(pl.multiple_of(head * 128, 128), 128)] = part[...]

    out[...] = dot(mixed[...], weights[...]).astype(BF16)


def output_columns(blocks, y, parts, weights):
    count = blocks.shape[0]

    def kernel(*refs):
        output_kernel(count, *refs)

    return pl.pallas_call(
        kernel,
        out_shape=jax.ShapeDtypeStruct((count * 512, 512), BF16),
        grid_spec=pltpu.PrefetchScalarGridSpec(
            num_scalar_prefetch=1,
            grid=(count,),
            in_specs=[pl.BlockSpec((512, 128), lambda s, info: (0, 0))] * 4
            + [pl.BlockSpec((512, 512), lambda s, info: (0, info[s]))],
            out_specs=pl.BlockSpec((512, 512), lambda s, info: (s, 0)),
            scratch_shapes=[pltpu.VMEM((512, 512), BF16)],
        ),
        compiler_params=pltpu.CompilerParams(vmem_limit_bytes=24 * 2**20),
        cost_estimate=pl.CostEstimate(
            flops=2 * 512**3 * count, bytes_accessed=count * 2**20, transcendentals=0
        ),
        name="output_columns",
    )(jnp.concatenate([blocks, y[None]]).astype(jnp.int32), *parts, weights)


def flip_seq(value, bit):
    return lax.ppermute(value, "seq", [(i, i ^ bit) for i in range(16)])


def per_device(
    tokens, boundary, heads_in, heads_out, gate_up, down_weight, widen, heads_in_two, heads_out_two
):
    seq_position = lax.axis_index("seq")
    me = lax.axis_index("blk")
    rows = tokens.shape[0]
    capacity = 512
    width = D1 // 8
    block_of = jnp.stack([((me ^ (4 * x)) & 4) | ((me + z) & 3) for x, z in PLACES])
    numbers = jnp.arange(8, dtype=jnp.int32)
    place_of = jnp.sum(
        jnp.where(block_of[None, :] == numbers[:, None], numbers[None, :], 0), axis=1
    )

    heads_in_flat = heads_in.transpose(1, 2, 0).reshape(3 * width, D1)
    core, y, half = seq_position & 1, (seq_position >> 1) & 3, seq_position >> 3
    piece = lax.dynamic_slice(widen, ((seq_position & 7) * 192, 0), (192, 512))

    near, opposite, diagonal = gather_blk(prepare(tokens))
    arrived = near[2 * SENT :]
    gates = later(gate_up, arrived)
    gate_flat, up_flat = lax.optimization_barrier((gates[:, 0, :], gates[:, 1, :]))
    info = later(jnp.concatenate([place_of, seq_position[None]]).astype(jnp.int32), gate_flat)
    qkv_near = project_one(heads_in_flat, near)
    qkv, edge = project_one(heads_in_flat, qkv_near, info, opposite, diagonal)
    halo = lax.ppermute(edge, "seq", [(i, i + 1) for i in range(15)])
    attended = window_attend(info, qkv, halo, window_attend(info, qkv))
    attn_near = dot(attended[: 4 * rows], heads_out).astype(BF16)
    attn_far = dot(attended[4 * rows :], heads_out).astype(BF16)
    opposite, diagonal = reduce_first(attn_far)

    marks_rows = jnp.pad(boundary.astype(BF16)[None, :], ((0, EXT - 1), (0, 512 - rows)))
    pieces = gather_blk(jnp.concatenate([piece, marks_rows], axis=0), qkv)
    pieces, marks = collect_pieces(*pieces, attended)
    pieces = lax.all_gather(
        pieces, "seq", axis=0, axis_index_groups=[[h * 8 + k for k in range(8)] for h in range(2)]
    ).reshape(8, 8, 192, 512)
    mid_stream = (
        tokens.astype(F32) + reduce_second(attn_near, opposite, diagonal)
    ).astype(BF16)

    normed_mid = normalize(mid_stream).astype(BF16)

    parts = gather_blk(normed_mid)
    mlp_near = mlp(gate_flat, up_flat, down_weight, parts[0])
    mlp_far = mlp(gate_flat, up_flat, down_weight, *parts[1:])
    counts = jnp.sum(marks, axis=1)
    before = jnp.sum(
        jnp.where(block_of[None, :] < block_of[:, None], counts[None, :], 0.0), axis=1
    )
    steps = jnp.arange(rows)
    running = dot(marks.astype(BF16), (steps[:, None] <= steps[None, :]).astype(BF16))
    slots = jnp.where(marks > 0.5, before[:, None] + running - 1.0, -1.0).astype(jnp.int32)
    span_count = jnp.sum(counts).astype(jnp.int32)
    targets = (block_of[:, None] * 64 + jnp.arange(64)[None, :]).reshape(capacity, 1)
    selector = (slots.reshape(1, 8 * rows) == targets).astype(BF16)
    placed = (
        dot(selector[:, : 4 * rows], mlp_near)
        + dot(selector[:, 4 * rows :], mlp_far)
        + dot(selector[:, :rows], mid_stream)
    ).astype(BF16)
    pooled_own = reduce_blk(placed[:256], placed[256:]).astype(BF16)
    pooled = gather_blk(pooled_own)

    validity = (jnp.arange(capacity, dtype=jnp.int32) < span_count).astype(F32)
    valid_rows = jnp.pad(
        validity.reshape(4, 128).astype(BF16), ((0, EXT - 4), (0, 0))
    )
    info_one = jnp.concatenate([block_of, y[None]]).astype(jnp.int32)
    chunks, wide_cols = project_two(
        info_one, pooled, pieces, heads_in_two.transpose(1, 0, 2), valid_rows
    )
    opposite, diagonal = reduce_first(later(mlp_far, chunks[0]))
    from_behind = turn_y(chunks[1], 1)
    from_ahead = turn_y(chunks[3], 3)
    from_opposite = turn_y(chunks[2], 2)
    mine = jnp.stack([chunks[0], from_ahead, from_opposite, from_behind])
    queries, own_kv = mine[:, :capacity, :128], mine[:, :, 128:]
    first_kv = lax.ppermute(own_kv, "seq", [(i, i + 8) for i in range(8)])
    info_two = jnp.stack([half, core, y]).astype(jnp.int32)
    running = causal_attend(True, info_two, queries, (own_kv, flip_seq(own_kv, 1)))
    first_kv = first_kv + running[1][0, 2, 0].astype(BF16)
    mixed = causal_attend(False, info_two, queries, (first_kv, flip_seq(first_kv, 1)), running)
    back = [mixed[0], turn_y(mixed[3], 3), turn_y(mixed[2], 2), turn_y(mixed[1], 1)]
    out_opposite = turn_z(output_columns(block_of[4:6], y, back, heads_out_two), 2)
    out_diagonal = flip_x(output_columns(block_of[6:], y, back, heads_out_two))
    level_one = (
        mid_stream.astype(F32)
        + reduce_second(later(mlp_near, mixed[0]), opposite, diagonal)
    ).astype(BF16)
    out_near = output_columns(later(block_of[:4], level_one), y, back, heads_out_two)
    level_two = (
        (wide_cols.astype(F32) + reduce_second(out_near, out_opposite, out_diagonal)) * validity[:, None]
    ).astype(BF16)
    return (level_one, level_two)


def solution(mesh):
    placed = (
        P(("seq", "blk"), None),
        P(("seq", "blk")),
        P(None, None, "blk"),
        P("blk", None),
        P(None, None, "blk"),
        P("blk", None),
        P(None, "blk"),
        P(None, None, "blk"),
        P("blk", None),
    )
    return jax.shard_map(
        per_device,
        mesh=mesh,
        in_specs=placed,
        out_specs=(P(("seq", "blk"), None), P("seq", "blk")),
        check_vma=False,
    )
```

profile of v0, /device:TPU:6, one launch (start us, length us, event | category | flops | bytes accessed | tf_op | source)
XLA Modules:
  0.0 347.6 jit_solution(15905349356067565463)
XLA Ops:
  9.2 4.0 %collective-permute-start = (bf16[128,1536]{1,0:T(8,128)(2,1)}, bf16[128,1536]{1,0:T(8,128)(2,1)S(1)}, u32[]{:S(2)}, u32[]{:S(2)}) collective-permute-start(bf16[128,1536]{1,0:T(8,128)(2,1)} %prepare.1), channel_id=1, source_target_pairs={{0,3},{1,0},{2,1},{3,2},{4,7},{5,4},{6,5},{7,6},{8,11},{9,8},{10,9... | collective-permute-start | bytes 1179656 | tf_op jit(solution)/shard_map/ppermute | solution.py:28
  15.4 3.2 collective-permute-start.15
  18.8 4.3 %collective-permute-done = bf16[128,1536]{1,0:T(8,128)(2,1)S(1)} collective-permute-done((bf16[128,1536]{1,0:T(8,128)(2,1)}, bf16[128,1536]{1,0:T(8,128)(2,1)S(1)}, u32[]{:S(2)}, u32[]{:S(2)}) %collective-permute-start) | collective-permute-done | bytes 393248 | tf_op jit(solution)/shard_map/ppermute | solution.py:28
  23.9 3.6 %collective-permute-done.2 = bf16[128,1536]{1,0:T(8,128)(2,1)S(1)} collective-permute-done((bf16[128,1536]{1,0:T(8,128)(2,1)}, bf16[128,1536]{1,0:T(8,128)(2,1)S(1)}, u32[]{:S(2)}, u32[]{:S(2)}) %collective-permute-start.2) | collective-permute-done | bytes 393248 | tf_op jit(solution)/shard_map/ppermute | solution.py:28
  35.5 10.3 %collective-permute-done.4.diagonal = bf16[256,1536]{1,0:T(8,128)(2,1)S(1)} collective-permute-done((bf16[256,1536]{1,0:T(8,128)(2,1)S(1)}, bf16[256,1536]{1,0:T(8,128)(2,1)S(1)}, u32[]{:S(2)}, u32[]{:S(2)}) %collective-permute-start.4) | collective-permute-done | bytes 786464 | tf_op jit(solution)/shard_map/ppermute | solution.py:24
  55.6 3.5 %window_late.1.before = bf16[1024,192]{1,0:T(8,128)(2,1)S(1)} custom-call(s32[9]{0:T(128)S(1)} %add_add_fusion.info, bf16[1024,576]{1,0:T(8,128)(2,1)S(1)} %get-tuple-element.13.qkv), custom_call_target="tpu_custom_call" | custom-call | flops 251658240 | bytes 2097152 | tf_op jit(solution)/shard_map/window_late/pallas_call | solution.py:143
  59.2 7.0 %collective-permute-done.5.halo = bf16[512,384]{1,0:T(8,128)(2,1)S(1)} collective-permute-done((bf16[512,384]{1,0:T(8,128)(2,1)S(1)}, bf16[512,384]{1,0:T(8,128)(2,1)S(1)}, u32[]{:S(2)}, u32[]{:S(2)}) %collective-permute-start.5) | collective-permute-done | bytes 393248 | tf_op jit(solution)/shard_map/ppermute | solution.py:532
  66.2 3.6 %window_early.1._ = bf16[1024,192]{1,0:T(8,128)(2,1)S(1)} custom-call(s32[9]{0:T(128)S(1)} %add_add_fusion.info, bf16[1024,576]{1,0:T(8,128)(2,1)S(1)} %get-tuple-element.13.qkv, bf16[512,384]{1,0:T(8,128)(2,1)S(1)} %collective-permute-done.5.halo, bf16[1024,192]{1,0:T(8,128)(2,1)S(1)} %window_late.1.before), custom_call_target="tpu_custom_call" | custom-call | flops 251658240 | bytes 2097152 | tf_op jit(solution)/shard_map/window_early/pallas_call | solution.py:143
  75.4 13.0 %collective-permute-done.6 = bf16[256,1536]{1,0:T(8,128)(2,1)S(1)} collective-permute-done((bf16[256,1536]{1,0:T(8,128)(2,1)S(1)}, bf16[256,1536]{1,0:T(8,128)(2,1)S(1)}, u32[]{:S(2)}, u32[]{:S(2)}) %collective-permute-start.6) | collective-permute-done | bytes 786464 | tf_op jit(solution)/shard_map/ppermute | solution.py:28
  89.5 3.8 %collective-permute-start.10 = (bf16[128,1536]{1,0:T(8,128)(2,1)S(1)}, bf16[128,1536]{1,0:T(8,128)(2,1)}, u32[]{:S(2)}, u32[]{:S(2)}) collective-permute-start(bf16[128,1536]{1,0:T(8,128)(2,1)S(1)} %get-tuple-element.33), channel_id=1, source_target_pairs={{0,3},{1,0},{2,1},{3,2},{4,7},{5,4},{6,5},{7,6},{8,11},{9,8},{10,9... | collective-permute-start | bytes 1179656 | tf_op jit(solution)/shard_map/ppermute | solution.py:28
  94.8 5.1 %collective-permute-done.10 = bf16[128,1536]{1,0:T(8,128)(2,1)} collective-permute-done((bf16[128,1536]{1,0:T(8,128)(2,1)S(1)}, bf16[128,1536]{1,0:T(8,128)(2,1)}, u32[]{:S(2)}, u32[]{:S(2)}) %collective-permute-start.10) | collective-permute-done | bytes 393248 | tf_op jit(solution)/shard_map/ppermute | solution.py:28
  101.4 3.9 %collective-permute-done.9 = bf16[128,1536]{1,0:T(8,128)(2,1)} collective-permute-done((bf16[128,1536]{1,0:T(8,128)(2,1)S(1)}, bf16[128,1536]{1,0:T(8,128)(2,1)}, u32[]{:S(2)}, u32[]{:S(2)}) %collective-permute-start.9) | collective-permute-done | bytes 393248 | tf_op jit(solution)/shard_map/ppermute | solution.py:28
  111.6 8.1 %collective-permute-done.12 = bf16[128,1536]{1,0:T(8,128)(2,1)S(1)} collective-permute-done((bf16[128,1536]{1,0:T(8,128)(2,1)S(1)}, bf16[128,1536]{1,0:T(8,128)(2,1)S(1)}, u32[]{:S(2)}, u32[]{:S(2)}) %collective-permute-start.12) | collective-permute-done | bytes 393248 | tf_op jit(solution)/shard_map/ppermute | solution.py:28
  119.7 5.5 %collective-permute-done.13 = bf16[128,1536]{1,0:T(8,128)(2,1)S(1)} collective-permute-done((bf16[128,1536]{1,0:T(8,128)(2,1)S(1)}, bf16[128,1536]{1,0:T(8,128)(2,1)S(1)}, u32[]{:S(2)}, u32[]{:S(2)}) %collective-permute-start.13) | collective-permute-done | bytes 393248 | tf_op jit(solution)/shard_map/ppermute | solution.py:28
  128.2 3.0 mlp.2
  131.2 9.3 %collective-permute-done.20.refs_1_ = bf16[256,1536]{1,0:T(8,128)(2,1)S(1)} collective-permute-done((bf16[256,1536]{1,0:T(8,128)(2,1)S(1)}, bf16[256,1536]{1,0:T(8,128)(2,1)S(1)}, u32[]{:S(2)}, u32[]{:S(2)}) %collective-permute-start.20) | collective-permute-done | bytes 786464 | tf_op jit(solution)/shard_map/ppermute | solution.py:24
  140.5 2.9 collective-permute-done.19.refs_0_
  150.5 9.4 %collective-permute-done.21 = bf16[128,1536]{1,0:T(8,128)(2,1)S(1)} collective-permute-done((bf16[128,1536]{1,0:T(8,128)(2,1)S(1)}, bf16[128,1536]{1,0:T(8,128)(2,1)S(1)}, u32[]{:S(2)}, u32[]{:S(2)}) %collective-permute-start.21) | collective-permute-done | bytes 393248 | tf_op jit(solution)/shard_map/ppermute | solution.py:28
  161.9 3.2 collective-permute-start.25
  168.8 3.3 collective-permute-done.25
  172.3 3.7 %collective-permute-start.27 = (bf16[64,1536]{1,0:T(8,128)(2,1)S(1)}, bf16[64,1536]{1,0:T(8,128)(2,1)S(1)}, u32[]{:S(2)}, u32[]{:S(2)}) collective-permute-start(bf16[64,1536]{1,0:T(8,128)(2,1)S(1)} %add_convert_fusion.10), channel_id=1, source_target_pairs={{0,3},{1,0},{2,1},{3,2},{4,7},{5,4},{6,5},{7,6},{8,11},{9,8},{10,9... | collective-permute-start | bytes 589832 | tf_op jit(solution)/shard_map/ppermute | solution.py:28
  176.3 2.9 collective-permute-done.27
  179.2 3.7 %collective-permute-done.28 = bf16[64,1536]{1,0:T(8,128)(2,1)S(1)} collective-permute-done((bf16[64,1536]{1,0:T(8,128)(2,1)S(1)}, bf16[64,1536]{1,0:T(8,128)(2,1)S(1)}, u32[]{:S(2)}, u32[]{:S(2)}) %collective-permute-start.28) | collective-permute-done | bytes 196640 | tf_op jit(solution)/shard_map/ppermute | solution.py:28
  187.9 4.5 %collective-permute-done.30.diagonal = bf16[128,1536]{1,0:T(8,128)(2,1)S(1)} collective-permute-done((bf16[128,1536]{1,0:T(8,128)(2,1)}, bf16[128,1536]{1,0:T(8,128)(2,1)S(1)}, u32[]{:S(2)}, u32[]{:S(2)}) %collective-permute-start.30) | collective-permute-done | bytes 393248 | tf_op jit(solution)/shard_map/ppermute | solution.py:24
  198.3 18.2 %project_two.1 = (bf16[4,528,384]{2,1,0:T(8,128)(2,1)S(1)}, bf16[512,512]{1,0:T(8,128)(2,1)S(1)}) custom-call(s32[9]{0:T(128)S(1)} %concatenate.73.info, bf16[256,1536]{1,0:T(8,128)(2,1)S(1)} %pad_maximum_fusion.10.near, bf16[128,1536]{1,0:T(8,128)(2,1)S(1)} %copy-done.12, bf16[128,1536]{1,0:T(8,128)(2,1)S(1)} %copy-done.10, ...), custom_call_target="tpu_custom_call" | custom-call | flops 12884901888 | bytes 29360128 | tf_op jit(solution)/shard_map/project_two/pallas_call | solution.py:314
  219.8 5.6 %collective-permute-done.31 = bf16[528,384]{1,0:T(8,128)(2,1)S(1)} collective-permute-done((bf16[528,384]{1,0:T(8,128)(2,1)S(1)}, bf16[528,384]{1,0:T(8,128)(2,1)S(1)}, u32[]{:S(2)}, u32[]{:S(2)}) %collective-permute-start.31) | collective-permute-done | bytes 405536 | tf_op jit(solution)/shard_map/ppermute | solution.py:463
  227.3 4.2 %collective-permute-done.33 = bf16[528,384]{1,0:T(8,128)(2,1)S(1)} collective-permute-done((bf16[528,384]{1,0:T(8,128)(2,1)S(1)}, bf16[528,384]{1,0:T(8,128)(2,1)S(1)}, u32[]{:S(2)}, u32[]{:S(2)}) %collective-permute-start.33) | collective-permute-done | bytes 405536 | tf_op jit(solution)/shard_map/ppermute | solution.py:463
  236.7 12.3 %causal_own.1 = (f32[4,128,512]{2,1,0:T(8,128)S(1)}, f32[4,8,512]{2,1,0:T(8,128)S(1)}) custom-call(s32[3]{0:T(128)S(1)} %add_add_fusion.1.info, bf16[4,512,128]{2,1,0:T(8,128)(2,1)S(1)} %pad_maximum_fusion.11.queries, bf16[4,528,256]{2,1,0:T(8,128)(2,1)S(1)} %pad_maximum_fusion.2.kv, bf16[4,528,256]{2,1,0:T(8,128)(2,1)} %collective-permute-done.35.other), custom_call_target="tpu_custom_call" | custom-call | flops 2415919104 | bytes 4194304 | tf_op jit(solution)/shard_map/causal_own/pallas_call | solution.py:439
  249.5 11.9 %collective-permute-done.34 = bf16[4,528,256]{2,1,0:T(8,128)(2,1)} collective-permute-done((bf16[4,528,256]{2,1,0:T(8,128)(2,1)S(1)}, bf16[4,528,256]{2,1,0:T(8,128)(2,1)}, u32[]{:S(2)}, u32[]{:S(2)}) %collective-permute-start.34) | collective-permute-done | bytes 1081376 | tf_op jit(solution)/shard_map/ppermute | solution.py:585
  266.2 16.6 %causal_first_half.1 = bf16[4,512,128]{2,1,0:T(8,128)(2,1)S(1)} custom-call(s32[3]{0:T(128)S(1)} %add_add_fusion.1.info, bf16[4,512,128]{2,1,0:T(8,128)(2,1)S(1)} %pad_maximum_fusion.11.queries, bf16[4,528,256]{2,1,0:T(8,128)(2,1)S(1)} %broadcast_add_fusion.2.kv, bf16[4,528,256]{2,1,0:T(8,128)(2,1)S(1)} %collective-permute-done.36.other, ...), custom_call_target="tpu_custom_call" | custom-call | flops 4294967296 | bytes 4194304 | tf_op jit(solution)/shard_map/causal_first_half/pallas_call | solution.py:439
  299.8 22.7 %collective-permute-done.40 = bf16[128,1536]{1,0:T(8,128)(2,1)S(1)} collective-permute-done((bf16[128,1536]{1,0:T(8,128)(2,1)S(1)}, bf16[128,1536]{1,0:T(8,128)(2,1)S(1)}, u32[]{:S(2)}, u32[]{:S(2)}) %collective-permute-start.40) | collective-permute-done | bytes 393248 | tf_op jit(solution)/shard_map/ppermute | solution.py:28
  330.8 6.8 %collective-permute-done.46 = bf16[512,512]{1,0:T(8,128)(2,1)S(1)} collective-permute-done((bf16[512,512]{1,0:T(8,128)(2,1)S(1)}, bf16[512,512]{1,0:T(8,128)(2,1)S(1)}, u32[]{:S(2)}, u32[]{:S(2)}) %collective-permute-start.46) | collective-permute-done | bytes 524320 | tf_op jit(solution)/shard_map/ppermute | solution.py:24
  (214 shorter events, 104.6 us)
Async XLA Ops:
  7.2 189.1 %all-gather.3.cloned.1.call-start = ((), (), s32[]{:S(2)}) async-start(), calls=%async_computation | async-start | bytes 14155776 | tf_op jit(solution)/shard_map/all_gather | solution.py:541
  9.2 13.9 %collective-permute-start = (bf16[128,1536]{1,0:T(8,128)(2,1)}, bf16[128,1536]{1,0:T(8,128)(2,1)S(1)}, u32[]{:S(2)}, u32[]{:S(2)}) collective-permute-start(bf16[128,1536]{1,0:T(8,128)(2,1)} %prepare.1), channel_id=1, source_target_pairs={{0,3},{1,0},{2,1},{3,2},{4,7},{5,4},{6,5},{7,6},{8,11},{9,8},{10,9... | collective-permute-start | bytes 1179656 | tf_op jit(solution)/shard_map/ppermute | solution.py:28
  13.3 15.6 %collective-permute-start.1 = (bf16[128,1536]{1,0:T(8,128)(2,1)}, bf16[128,1536]{1,0:T(8,128)(2,1)S(1)}, u32[]{:S(2)}, u32[]{:S(2)}) collective-permute-start(bf16[128,1536]{1,0:T(8,128)(2,1)} %prepare.1), channel_id=1, source_target_pairs={{0,4},{1,5},{2,6},{3,7},{4,0},{5,1},{6,2},{7,3},{8,12},{9,13},{10,... | collective-permute-start | bytes 1179656 | tf_op jit(solution)/shard_map/ppermute | solution.py:24
  14.1 13.5 %collective-permute-start.2 = (bf16[128,1536]{1,0:T(8,128)(2,1)}, bf16[128,1536]{1,0:T(8,128)(2,1)S(1)}, u32[]{:S(2)}, u32[]{:S(2)}) collective-permute-start(bf16[128,1536]{1,0:T(8,128)(2,1)} %prepare.1), channel_id=1, source_target_pairs={{0,1},{1,2},{2,3},{3,0},{4,5},{5,6},{6,7},{7,4},{8,9},{9,10},{10,1... | collective-permute-start | bytes 1179656 | tf_op jit(solution)/shard_map/ppermute | solution.py:28
  15.4 34.2 %collective-permute-start.15 = (bf16[208,512]{1,0:T(8,128)(2,1)S(1)}, bf16[208,512]{1,0:T(8,128)(2,1)S(1)}, u32[]{:S(2)}, u32[]{:S(2)}) collective-permute-start(bf16[208,512]{1,0:T(8,128)(2,1)S(1)} %pad_maximum_fusion.14), channel_id=1, source_target_pairs={{0,3},{1,0},{2,1},{3,2},{4,7},{5,4},{6,5},{7,6},{8,11},{9,8},{10,9... | collective-permute-start | bytes 638984 | tf_op jit(solution)/shard_map/ppermute | solution.py:28
  18.6 31.0 %collective-permute-start.16 = (bf16[208,512]{1,0:T(8,128)(2,1)S(1)}, bf16[208,512]{1,0:T(8,128)(2,1)}, u32[]{:S(2)}, u32[]{:S(2)}) collective-permute-start(bf16[208,512]{1,0:T(8,128)(2,1)S(1)} %pad_maximum_fusion.14), channel_id=1, source_target_pairs={{0,1},{1,2},{2,3},{3,0},{4,5},{5,6},{6,7},{7,4},{8,9},{9,10},{10,1... | collective-permute-start | bytes 638984 | tf_op jit(solution)/shard_map/ppermute | solution.py:28
  23.1 28.4 %collective-permute-start.14 = (bf16[208,512]{1,0:T(8,128)(2,1)S(1)}, bf16[208,512]{1,0:T(8,128)(2,1)S(1)}, u32[]{:S(2)}, u32[]{:S(2)}) collective-permute-start(bf16[208,512]{1,0:T(8,128)(2,1)S(1)} %pad_maximum_fusion.14), channel_id=1, source_target_pairs={{0,4},{1,5},{2,6},{3,7},{4,0},{5,1},{6,2},{7,3},{8,12},{9,13},{10,... | collective-permute-start | bytes 638984 | tf_op jit(solution)/shard_map/ppermute | solution.py:24
  27.6 18.2 %collective-permute-start.4 = (bf16[256,1536]{1,0:T(8,128)(2,1)S(1)}, bf16[256,1536]{1,0:T(8,128)(2,1)S(1)}, u32[]{:S(2)}, u32[]{:S(2)}) collective-permute-start(bf16[256,1536]{1,0:T(8,128)(2,1)S(1)} %pad_maximum_fusion.7), channel_id=1, source_target_pairs={{0,4},{1,5},{2,6},{3,7},{4,0},{5,1},{6,2},{7,3},{8,12},{9,13},{10,... | collective-permute-start | bytes 2359304 | tf_op jit(solution)/shard_map/ppermute | solution.py:24
  29.0 17.4 %collective-permute-start.3 = (bf16[256,1536]{1,0:T(8,128)(2,1)S(1)}, bf16[256,1536]{1,0:T(8,128)(2,1)S(1)}, u32[]{:S(2)}, u32[]{:S(2)}) collective-permute-start(bf16[256,1536]{1,0:T(8,128)(2,1)S(1)} %pad_maximum_fusion.6), channel_id=1, source_target_pairs={{0,2},{1,3},{2,0},{3,1},{4,6},{5,7},{6,4},{7,5},{8,10},{9,11},{10,... | collective-permute-start | bytes 2359304 | tf_op jit(solution)/shard_map/ppermute | solution.py:28
  50.6 19.2 %collective-permute-start.18 = (bf16[416,512]{1,0:T(8,128)(2,1)S(1)}, bf16[416,512]{1,0:T(8,128)(2,1)S(1)}, u32[]{:S(2)}, u32[]{:S(2)}) collective-permute-start(bf16[416,512]{1,0:T(8,128)(2,1)S(1)} %maximum_add_fusion.1), channel_id=1, source_target_pairs={{0,4},{1,5},{2,6},{3,7},{4,0},{5,1},{6,2},{7,3},{8,12},{9,13},{10,... | collective-permute-start | bytes 1277960 | tf_op jit(solution)/shard_map/ppermute | solution.py:24
  51.6 18.2 %collective-permute-start.17 = (bf16[416,512]{1,0:T(8,128)(2,1)S(1)}, bf16[416,512]{1,0:T(8,128)(2,1)S(1)}, u32[]{:S(2)}, u32[]{:S(2)}) collective-permute-start(bf16[416,512]{1,0:T(8,128)(2,1)S(1)} %maximum_add_fusion), channel_id=1, source_target_pairs={{0,2},{1,3},{2,0},{3,1},{4,6},{5,7},{6,4},{7,5},{8,10},{9,11},{10,... | collective-permute-start | bytes 1277960 | tf_op jit(solution)/shard_map/ppermute | solution.py:28
  53.5 12.7 %collective-permute-start.5 = (bf16[512,384]{1,0:T(8,128)(2,1)S(1)}, bf16[512,384]{1,0:T(8,128)(2,1)S(1)}, u32[]{:S(2)}, u32[]{:S(2)}) collective-permute-start(bf16[512,384]{1,0:T(8,128)(2,1)S(1)} %get-tuple-element.14), channel_id=1, source_target_pairs={{0,8},{8,16},{16,24},{24,32},{32,40},{40,48},{48,56},{56,64},{64,7... | collective-permute-start | bytes 1179656 | tf_op jit(solution)/shard_map/ppermute | solution.py:532
  71.8 16.6 %collective-permute-start.6 = (bf16[256,1536]{1,0:T(8,128)(2,1)S(1)}, bf16[256,1536]{1,0:T(8,128)(2,1)S(1)}, u32[]{:S(2)}, u32[]{:S(2)}) collective-permute-start(bf16[256,1536]{1,0:T(8,128)(2,1)S(1)} %get-tuple-element.49), channel_id=1, source_target_pairs={{0,2},{1,3},{2,0},{3,1},{4,6},{5,7},{6,4},{7,5},{8,10},{9,11},{10,... | collective-permute-start | bytes 2359304 | tf_op jit(solution)/shard_map/ppermute | solution.py:28
  74.4 14.8 %collective-permute-start.8 = (bf16[256,1536]{1,0:T(8,128)(2,1)S(1)}, bf16[256,1536]{1,0:T(8,128)(2,1)S(1)}, u32[]{:S(2)}, u32[]{:S(2)}) collective-permute-start(bf16[256,1536]{1,0:T(8,128)(2,1)S(1)} %get-tuple-element.50), channel_id=1, source_target_pairs={{0,4},{1,5},{2,6},{3,7},{4,0},{5,1},{6,2},{7,3},{8,12},{9,13},{10,... | collective-permute-start | bytes 2359304 | tf_op jit(solution)/shard_map/ppermute | solution.py:24
  94.0 11.3 %collective-permute-start.9 = (bf16[128,1536]{1,0:T(8,128)(2,1)S(1)}, bf16[128,1536]{1,0:T(8,128)(2,1)}, u32[]{:S(2)}, u32[]{:S(2)}) collective-permute-start(bf16[128,1536]{1,0:T(8,128)(2,1)S(1)} %get-tuple-element.32), channel_id=1, source_target_pairs={{0,1},{1,2},{2,3},{3,0},{4,5},{5,6},{6,7},{7,4},{8,9},{9,10},{10,1... | collective-permute-start | bytes 1179656 | tf_op jit(solution)/shard_map/ppermute | solution.py:28
  107.5 12.1 %collective-permute-start.12 = (bf16[128,1536]{1,0:T(8,128)(2,1)S(1)}, bf16[128,1536]{1,0:T(8,128)(2,1)S(1)}, u32[]{:S(2)}, u32[]{:S(2)}) collective-permute-start(bf16[128,1536]{1,0:T(8,128)(2,1)S(1)} %fusion.7), channel_id=1, source_target_pairs={{0,3},{1,0},{2,1},{3,2},{4,7},{5,4},{6,5},{7,6},{8,11},{9,8},{10,9... | collective-permute-start | bytes 1179656 | tf_op jit(solution)/shard_map/ppermute | solution.py:28
  107.6 17.5 %collective-permute-start.13 = (bf16[128,1536]{1,0:T(8,128)(2,1)S(1)}, bf16[128,1536]{1,0:T(8,128)(2,1)S(1)}, u32[]{:S(2)}, u32[]{:S(2)}) collective-permute-start(bf16[128,1536]{1,0:T(8,128)(2,1)S(1)} %fusion.7), channel_id=1, source_target_pairs={{0,1},{1,2},{2,3},{3,0},{4,5},{5,6},{6,7},{7,4},{8,9},{9,10},{10,1... | collective-permute-start | bytes 1179656 | tf_op jit(solution)/shard_map/ppermute | solution.py:28
  109.9 15.3 %collective-permute-start.11 = (bf16[128,1536]{1,0:T(8,128)(2,1)S(1)}, bf16[128,1536]{1,0:T(8,128)(2,1)S(1)}, u32[]{:S(2)}, u32[]{:S(2)}) collective-permute-start(bf16[128,1536]{1,0:T(8,128)(2,1)S(1)} %fusion.7), channel_id=1, source_target_pairs={{0,4},{1,5},{2,6},{3,7},{4,0},{5,1},{6,2},{7,3},{8,12},{9,13},{10,... | collective-permute-start | bytes 1179656 | tf_op jit(solution)/shard_map/ppermute | solution.py:24
  125.2 15.3 %collective-permute-start.20 = (bf16[256,1536]{1,0:T(8,128)(2,1)S(1)}, bf16[256,1536]{1,0:T(8,128)(2,1)S(1)}, u32[]{:S(2)}, u32[]{:S(2)}) collective-permute-start(bf16[256,1536]{1,0:T(8,128)(2,1)S(1)} %pad_maximum_fusion.9), channel_id=1, source_target_pairs={{0,4},{1,5},{2,6},{3,7},{4,0},{5,1},{6,2},{7,3},{8,12},{9,13},{10,... | collective-permute-start | bytes 2359304 | tf_op jit(solution)/shard_map/ppermute | solution.py:24
  125.3 18.0 %collective-permute-start.19 = (bf16[256,1536]{1,0:T(8,128)(2,1)S(1)}, bf16[256,1536]{1,0:T(8,128)(2,1)S(1)}, u32[]{:S(2)}, u32[]{:S(2)}) collective-permute-start(bf16[256,1536]{1,0:T(8,128)(2,1)S(1)} %pad_maximum_fusion.8), channel_id=1, source_target_pairs={{0,2},{1,3},{2,0},{3,1},{4,6},{5,7},{6,4},{7,5},{8,10},{9,11},{10,... | collective-permute-start | bytes 2359304 | tf_op jit(solution)/shard_map/ppermute | solution.py:28
  148.3 11.6 %collective-permute-start.21 = (bf16[128,1536]{1,0:T(8,128)(2,1)S(1)}, bf16[128,1536]{1,0:T(8,128)(2,1)S(1)}, u32[]{:S(2)}, u32[]{:S(2)}) collective-permute-start(bf16[128,1536]{1,0:T(8,128)(2,1)S(1)} %get-tuple-element.46), channel_id=1, source_target_pairs={{0,2},{1,3},{2,0},{3,1},{4,6},{5,7},{6,4},{7,5},{8,10},{9,11},{10,... | collective-permute-start | bytes 1179656 | tf_op jit(solution)/shard_map/ppermute | solution.py:28
  148.4 11.5 %collective-permute-start.23 = (bf16[128,1536]{1,0:T(8,128)(2,1)S(1)}, bf16[128,1536]{1,0:T(8,128)(2,1)S(1)}, u32[]{:S(2)}, u32[]{:S(2)}) collective-permute-start(bf16[128,1536]{1,0:T(8,128)(2,1)S(1)} %get-tuple-element.47), channel_id=1, source_target_pairs={{0,4},{1,5},{2,6},{3,7},{4,0},{5,1},{6,2},{7,3},{8,12},{9,13},{10,... | collective-permute-start | bytes 1179656 | tf_op jit(solution)/shard_map/ppermute | solution.py:24
  217.7 13.7 %collective-permute-start.33 = (bf16[528,384]{1,0:T(8,128)(2,1)S(1)}, bf16[528,384]{1,0:T(8,128)(2,1)S(1)}, u32[]{:S(2)}, u32[]{:S(2)}) collective-permute-start(bf16[528,384]{1,0:T(8,128)(2,1)S(1)} %get-tuple-element.39), channel_id=1, source_target_pairs={{0,16},{8,24},{16,32},{24,40},{32,48},{40,56},{48,0},{56,8},{64,80... | collective-permute-start | bytes 1216520 | tf_op jit(solution)/shard_map/ppermute | solution.py:463
  232.2 29.2 %collective-permute-start.34 = (bf16[4,528,256]{2,1,0:T(8,128)(2,1)S(1)}, bf16[4,528,256]{2,1,0:T(8,128)(2,1)}, u32[]{:S(2)}, u32[]{:S(2)}) collective-permute-start(bf16[4,528,256]{2,1,0:T(8,128)(2,1)S(1)} %pad_maximum_fusion.2.kv), channel_id=1, source_target_pairs={{0,64},{8,72},{16,80},{24,88},{32,96},{40,104},{48,112},{56,120},{... | collective-permute-start | bytes 3244040 | tf_op jit(solution)/shard_map/ppermute | solution.py:585
  263.7 22.5 %collective-permute-start.37 = (bf16[256,1536]{1,0:T(8,128)(2,1)S(1)}, bf16[256,1536]{1,0:T(8,128)(2,1)S(1)}, u32[]{:S(2)}, u32[]{:S(2)}) collective-permute-start(bf16[256,1536]{1,0:T(8,128)(2,1)S(1)} %get-tuple-element.43), channel_id=1, source_target_pairs={{0,2},{1,3},{2,0},{3,1},{4,6},{5,7},{6,4},{7,5},{8,10},{9,11},{10,... | collective-permute-start | bytes 2359304 | tf_op jit(solution)/shard_map/ppermute | solution.py:28
  263.8 22.4 %collective-permute-start.39 = (bf16[256,1536]{1,0:T(8,128)(2,1)S(1)}, bf16[256,1536]{1,0:T(8,128)(2,1)S(1)}, u32[]{:S(2)}, u32[]{:S(2)}) collective-permute-start(bf16[256,1536]{1,0:T(8,128)(2,1)S(1)} %get-tuple-element.44), channel_id=1, source_target_pairs={{0,4},{1,5},{2,6},{3,7},{4,0},{5,1},{6,2},{7,3},{8,12},{9,13},{10,... | collective-permute-start | bytes 2359304 | tf_op jit(solution)/shard_map/ppermute | solution.py:24
  286.5 13.3 %collective-permute-start.38 = (bf16[128,1536]{1,0:T(8,128)(2,1)S(1)}, bf16[128,1536]{1,0:T(8,128)(2,1)S(1)}, u32[]{:S(2)}, u32[]{:S(2)}) collective-permute-start(bf16[128,1536]{1,0:T(8,128)(2,1)S(1)} %get-tuple-element.42), channel_id=1, source_target_pairs={{0,4},{1,5},{2,6},{3,7},{4,0},{5,1},{6,2},{7,3},{8,12},{9,13},{10,... | collective-permute-start | bytes 1179656 | tf_op jit(solution)/shard_map/ppermute | solution.py:24
  288.5 34.0 %collective-permute-start.40 = (bf16[128,1536]{1,0:T(8,128)(2,1)S(1)}, bf16[128,1536]{1,0:T(8,128)(2,1)S(1)}, u32[]{:S(2)}, u32[]{:S(2)}) collective-permute-start(bf16[128,1536]{1,0:T(8,128)(2,1)S(1)} %get-tuple-element.30), channel_id=1, source_target_pairs={{0,1},{1,2},{2,3},{3,0},{4,5},{5,6},{6,7},{7,4},{8,9},{9,10},{10,1... | collective-permute-start | bytes 1179656 | tf_op jit(solution)/shard_map/ppermute | solution.py:28
  289.2 33.3 %collective-permute-start.41 = (bf16[128,1536]{1,0:T(8,128)(2,1)S(1)}, bf16[128,1536]{1,0:T(8,128)(2,1)S(1)}, u32[]{:S(2)}, u32[]{:S(2)}) collective-permute-start(bf16[128,1536]{1,0:T(8,128)(2,1)S(1)} %get-tuple-element.31), channel_id=1, source_target_pairs={{0,3},{1,0},{2,1},{3,2},{4,7},{5,4},{6,5},{7,6},{8,11},{9,8},{10,9... | collective-permute-start | bytes 1179656 | tf_op jit(solution)/shard_map/ppermute | solution.py:28
  295.0 31.9 %collective-permute-start.45 = (bf16[1024,512]{1,0:T(8,128)(2,1)S(1)}, bf16[1024,512]{1,0:T(8,128)(2,1)S(1)}, u32[]{:S(2)}, u32[]{:S(2)}) collective-permute-start(bf16[1024,512]{1,0:T(8,128)(2,1)S(1)} %output_columns.4), channel_id=1, source_target_pairs={{0,2},{1,3},{2,0},{3,1},{4,6},{5,7},{6,4},{7,5},{8,10},{9,11},{10,... | collective-permute-start | bytes 3145736 | tf_op jit(solution)/shard_map/ppermute | solution.py:28
  299.4 27.4 %collective-permute-start.47 = (bf16[1024,512]{1,0:T(8,128)(2,1)S(1)}, bf16[1024,512]{1,0:T(8,128)(2,1)S(1)}, u32[]{:S(2)}, u32[]{:S(2)}) collective-permute-start(bf16[1024,512]{1,0:T(8,128)(2,1)S(1)} %output_columns.5), channel_id=1, source_target_pairs={{0,4},{1,5},{2,6},{3,7},{4,0},{5,1},{6,2},{7,3},{8,12},{9,13},{10,... | collective-permute-start | bytes 3145736 | tf_op jit(solution)/shard_map/ppermute | solution.py:24
  327.4 11.4 %collective-permute-start.48 = (bf16[512,512]{1,0:T(8,128)(2,1)S(1)}, bf16[512,512]{1,0:T(8,128)(2,1)S(1)}, u32[]{:S(2)}, u32[]{:S(2)}) collective-permute-start(bf16[512,512]{1,0:T(8,128)(2,1)S(1)} %get-tuple-element.26), channel_id=1, source_target_pairs={{0,1},{1,2},{2,3},{3,0},{4,5},{5,6},{6,7},{7,4},{8,9},{9,10},{10,1... | collective-permute-start | bytes 1572872 | tf_op jit(solution)/shard_map/ppermute | solution.py:28
  (49 other events, 367.1 us)
Sparse Core Ops, SparseCore 0:
  71.2 65.1 all-gather.2
where the time goes:
time: 354 us; the launch traced here: 348 us
  waiting for transfers between devices  163 us (46%)
  Pallas kernels  72.5 us (20%)
  starting transfers between devices  57.1 us (16%)
  between operations  19.8 us (6%)
  local copies, waits for them, and re-layouts  16.2 us (5%)
  other arithmetic  15.6 us (4%)
  matrix products  3.73 us (1%)
    ppermute x24, waiting for transfers between devices, turn_z(): lax.ppermute(value, 'blk', [(i, i & 4 | i + steps & 3) for i in range(8)])  94.8 us
    ppermute x16, waiting for transfers between devices, flip_x(): return lax.ppermute(value, 'blk', [(i, i ^ 4) for i in range(8)])  34.7 us
    ppermute x24, starting transfers between devices, turn_z(): lax.ppermute(value, 'blk', [(i, i & 4 | i + steps & 3) for i in range(8)])  33.8 us
    pallas_call x2, Pallas kernels, causal_attend(): pl.pallas_call(kernel, out_shape=out_shape, grid_spec=pltpu.PrefetchScala...  28.8 us
    pallas_call x1, Pallas kernels, project_two(): pl.pallas_call(project_kernel, out_shape=(jax.ShapeDtypeStruct((4, 512 +...  18.2 us
    ppermute x16, starting transfers between devices, flip_x(): return lax.ppermute(value, 'blk', [(i, i ^ 4) for i in range(8)])  15.3 us
    ppermute x6, waiting for transfers between devices, turn_y(): lax.ppermute(value, 'seq', [(i, i & 9 | i + 2 * steps & 6) for i in range...  13.8 us
    ppermute x1, waiting for transfers between devices, per_device(): first_kv = lax.ppermute(own_kv, 'seq', [(i, i + 8) for i in range(8)])  11.9 us
  transfers between devices with their start and end apart: 51, of which 32 were waited for; matrix products, arithmetic and copies ran while one was open for 6% of the time, Pallas kernels for 15%

commit v1 on v0

--- a/solution.py
+++ b/solution.py
@@ -344,7 +344,7 @@
     )(info, *pooled, pieces, weights, valid)
 
 
-def causal_kernel(own_part, info, queries, kv_pair, start, start_stats, out, out_stats, keys, values, even, odd):
+def causal_kernel(mode, info, queries, kv_parts, start, start_stats, out, out_stats, keys, values, even, odd):
     half, core, y = info[0], info[1], info[2]
     slot = pl.program_id(0)
     own_pair = (y + slot) & 3
@@ -354,7 +354,7 @@
         def prepare(block, _):
             row = lax.broadcasted_iota(jnp.int32, (512, 128), 0).astype(F32)
             lane = lax.broadcasted_iota(jnp.int32, (512, 128), 1)
-            for which, kv in enumerate(kv_pair):
+            for which, kv in enumerate(kv_parts):
                 count = jnp.sum(kv[block, 512 : 512 + EXT, :128].astype(F32))
                 invalid = (lane == 0) & (row >= count)
                 keys[which * 4 + block, :, :128] = kv[block, :512, :128]
@@ -368,6 +368,8 @@
     query = jnp.concatenate([queries[0], jnp.where(lane == 0, 1.0, 0.0).astype(BF16)], axis=1)
 
     def block_of(pair, which):
+        if mode != "own":
+            return pair * 2 + which
         return (which ^ core) * 4 + ((pair - y) & 3)
 
     def scores_of(pair, which):
@@ -394,48 +396,50 @@
         odd[...] = scores_of(pair, 1)
         carry = absorb(even[...], pair, 0, carry, edge)
         if not edge:
-            even[...] = scores_of((pair + 1) & 3, 0)
+            even[...] = scores_of((pair + 1) & (3 if mode == "own" else 1), 0)
         return absorb(odd[...], pair, 1, carry, edge)
 
-    if own_part:
+    if mode == "own":
         carry = (
             jnp.full((1, 512), MASKED, F32), jnp.zeros((1, 512), F32), jnp.zeros((128, 512), F32)
         )
         carry = lax.fori_loop(0, own_pair, both, carry)
-        largest, total, sums = both(own_pair, carry, True)
+        carry = both(own_pair, carry, True)
+    else:
+        carry = (start_stats[0, 0:1], start_stats[0, 1:2], start[0])
+        carry = lax.fori_loop(0, half * 2, both, carry)
+    largest, total, sums = carry
+    if mode == "last":
+        out[0] = (sums / total).T.astype(BF16)
+    else:
         out[0] = sums
         out_stats[0] = jnp.concatenate([largest, total, jnp.zeros((6, 512), F32)], axis=0)
-    else:
-        carry = (start_stats[0, 0:1], start_stats[0, 1:2], start[0])
-        _, total, sums = lax.fori_loop(0, half * 4, both, carry)
-        out[0] = (sums / total).T.astype(BF16)
-
-
-def causal_attend(own_part, info, queries, kv_pair, start=None):
+
+
+def causal_attend(mode, info, queries, kv_parts, start=()):
     def by_slot(*shape):
         return pl.BlockSpec((1, *shape), lambda s, info: (s, 0, 0))
 
     sums_shape = jax.ShapeDtypeStruct((4, 128, 512), F32)
     stats_shape = jax.ShapeDtypeStruct((4, 8, 512), F32)
     whole = pl.BlockSpec((4, 512 + EXT, 256), lambda s, info: (0, 0, 0))
-    in_specs = [by_slot(512, 128), whole, whole]
-    operands = [queries, *kv_pair]
-    if own_part:
-        def kernel(info, queries, kv, other, out, out_stats, *scratch):
-            causal_kernel(True, info, queries, (kv, other), None, None, out, out_stats, *scratch)
-
-        out_shape = (sums_shape, stats_shape)
-        out_specs = (by_slot(128, 512), by_slot(8, 512))
-        tiles = 18
+    in_specs = [by_slot(512, 128)] + [whole] * len(kv_parts)
+    out_shape, out_specs = (sums_shape, stats_shape), (by_slot(128, 512), by_slot(8, 512))
+    if mode == "own":
+        def kernel(info, queries, kv, other, *rest):
+            causal_kernel(mode, info, queries, (kv, other), None, None, *rest)
+    elif mode == "more":
+        def kernel(info, queries, kv, *rest):
+            causal_kernel(mode, info, queries, (kv,), *rest)
     else:
-        def kernel(info, queries, kv, other, start, start_stats, out, *scratch):
-            causal_kernel(False, info, queries, (kv, other), start, start_stats, out, None, *scratch)
-
-        out_shape = jax.ShapeDtypeStruct((4, 512, 128), BF16)
-        out_specs = by_slot(512, 128)
+        def kernel(info, queries, kv, start, start_stats, out, *scratch):
+            causal_kernel(mode, info, queries, (kv,), start, start_stats, out, None, *scratch)
+
+        out_shape, out_specs = jax.ShapeDtypeStruct((4, 512, 128), BF16), by_slot(512, 128)
+    if start:
         in_specs += [by_slot(128, 512), by_slot(8, 512)]
-        operands += list(start)
-        tiles = 32
+    operands = [queries, *kv_parts, *start]
+    tiles = 18 if mode == "own" else 16
     return pl.pallas_call(
         kernel,
         out_shape=out_shape,
@@ -455,7 +459,7 @@
         cost_estimate=pl.CostEstimate(
             flops=tiles * 512 * 512 * 512, bytes_accessed=4 * 2**20, transcendentals=tiles * 2**18
         ),
-        name="causal_own" if own_part else "causal_first_half",
+        name="causal_" + mode,
     )(info, *operands)
 
 
@@ -584,9 +588,12 @@
     queries, own_kv = mine[:, :capacity, :128], mine[:, :, 128:]
     first_kv = lax.ppermute(own_kv, "seq", [(i, i + 8) for i in range(8)])
     info_two = jnp.stack([half, core, y]).astype(jnp.int32)
-    running = causal_attend(True, info_two, queries, (own_kv, flip_seq(own_kv, 1)))
-    first_kv = first_kv + running[1][0, 2, 0].astype(BF16)
-    mixed = causal_attend(False, info_two, queries, (first_kv, flip_seq(first_kv, 1)), running)
+    running = causal_attend("own", info_two, queries, (own_kv, flip_seq(own_kv, 1)))
+    unread = jnp.broadcast_to(running[1][0:1, 2:3, :128], (1, EXT, 128)).astype(BF16)
+    first_kv = lax.dynamic_update_slice(first_kv, unread, (0, capacity, 128))
+    first_other = flip_seq(first_kv, 1)
+    running = causal_attend("more", info_two, queries, (first_kv,), running)
+    mixed = causal_attend("last", info_two, queries, (first_other,), running)
     back = [mixed[0], turn_y(mixed[3], 3), turn_y(mixed[2], 2), turn_y(mixed[1], 1)]
     out_opposite = turn_z(output_columns(block_of[4:6], y, back, heads_out_two), 2)
     out_diagonal = flip_x(output_columns(block_of[6:], y, back, heads_out_two))

time: 354 us -> 356 us (level)
  Pallas kernels: 72.5 us -> 76.1 us
    ppermute x24, waiting for transfers between devices: 94.8 us -> 89 us  [turn_z(): lax.ppermute(value, 'blk', [(i, i & 4 | i + steps & 3) for i in range(8)])]
    ppermute x16, waiting for transfers between devices: 34.7 us -> 38.3 us  [flip_x(): return lax.ppermute(value, 'blk', [(i, i ^ 4) for i in range(8)])]
    pallas_call x2 -> x3, Pallas kernels: 28.8 us -> 32.4 us  [causal_attend(): pl.pallas_call(kernel, out_shape=out_shape, grid_spec=pltpu.PrefetchScala...]
  transfers between devices with their start and end apart: 51 -> 51, of which waited for: 32 -> 34; matrix products, arithmetic and copies ran while one was open for 6% -> 6% of each run, Pallas kernels for 15% -> 16%
where the time goes in v1:
time: 356 us; the launch traced here: 350 us
  waiting for transfers between devices  163 us (46%)
  Pallas kernels  76.1 us (21%)
  starting transfers between devices  57.8 us (16%)
  between operations  19.8 us (6%)
  local copies, waits for them, and re-layouts  16.2 us (5%)
  other arithmetic  13.7 us (4%)
  matrix products  3.73 us (1%)
    ppermute x24, waiting for transfers between devices, turn_z(): lax.ppermute(value, 'blk', [(i, i & 4 | i + steps & 3) for i in range(8)])  89 us
    ppermute x16, waiting for transfers between devices, flip_x(): return lax.ppermute(value, 'blk', [(i, i ^ 4) for i in range(8)])  38.3 us
    ppermute x24, starting transfers between devices, turn_z(): lax.ppermute(value, 'blk', [(i, i & 4 | i + steps & 3) for i in range(8)])  34.7 us
    pallas_call x3, Pallas kernels, causal_attend(): pl.pallas_call(kernel, out_shape=out_shape, grid_spec=pltpu.PrefetchScala...  32.4 us
    pallas_call x1, Pallas kernels, project_two(): pl.pallas_call(project_kernel, out_shape=(jax.ShapeDtypeStruct((4, 512 +...  18.2 us
    ppermute x6, waiting for transfers between devices, turn_y(): lax.ppermute(value, 'seq', [(i, i & 9 | i + 2 * steps & 6) for i in range...  15.5 us
    ppermute x16, starting transfers between devices, flip_x(): return lax.ppermute(value, 'blk', [(i, i ^ 4) for i in range(8)])  15.1 us
    ppermute x1, waiting for transfers between devices, per_device(): first_kv = lax.ppermute(own_kv, 'seq', [(i, i + 8) for i in range(8)])  12.6 us
  transfers between devices with their start and end apart: 51, of which 34 were waited for; matrix products, arithmetic and copies ran while one was open for 6% of the time, Pallas kernels for 16%

profile of v1, /device:TPU:6, one launch (start us, length us, event | category | flops | bytes accessed | tf_op | source)
XLA Modules:
  0.0 349.8 jit_solution(227408970423368218)
XLA Ops:
  9.2 4.0 %collective-permute-start = (bf16[128,1536]{1,0:T(8,128)(2,1)}, bf16[128,1536]{1,0:T(8,128)(2,1)S(1)}, u32[]{:S(2)}, u32[]{:S(2)}) collective-permute-start(bf16[128,1536]{1,0:T(8,128)(2,1)} %prepare.1), channel_id=1, source_target_pairs={{0,3},{1,0},{2,1},{3,2},{4,7},{5,4},{6,5},{7,6},{8,11},{9,8},{10,9... | collective-permute-start | bytes 1179656 | tf_op jit(solution)/shard_map/ppermute | solution.py:28
  15.4 3.2 collective-permute-start.15
  18.8 4.3 %collective-permute-done = bf16[128,1536]{1,0:T(8,128)(2,1)S(1)} collective-permute-done((bf16[128,1536]{1,0:T(8,128)(2,1)}, bf16[128,1536]{1,0:T(8,128)(2,1)S(1)}, u32[]{:S(2)}, u32[]{:S(2)}) %collective-permute-start) | collective-permute-done | bytes 393248 | tf_op jit(solution)/shard_map/ppermute | solution.py:28
  23.9 3.6 %collective-permute-done.2 = bf16[128,1536]{1,0:T(8,128)(2,1)S(1)} collective-permute-done((bf16[128,1536]{1,0:T(8,128)(2,1)}, bf16[128,1536]{1,0:T(8,128)(2,1)S(1)}, u32[]{:S(2)}, u32[]{:S(2)}) %collective-permute-start.2) | collective-permute-done | bytes 393248 | tf_op jit(solution)/shard_map/ppermute | solution.py:28
  35.5 10.3 %collective-permute-done.4.diagonal = bf16[256,1536]{1,0:T(8,128)(2,1)S(1)} collective-permute-done((bf16[256,1536]{1,0:T(8,128)(2,1)S(1)}, bf16[256,1536]{1,0:T(8,128)(2,1)S(1)}, u32[]{:S(2)}, u32[]{:S(2)}) %collective-permute-start.4) | collective-permute-done | bytes 786464 | tf_op jit(solution)/shard_map/ppermute | solution.py:24
  55.6 3.5 %window_late.1.before = bf16[1024,192]{1,0:T(8,128)(2,1)S(1)} custom-call(s32[9]{0:T(128)S(1)} %add_add_fusion.info, bf16[1024,576]{1,0:T(8,128)(2,1)S(1)} %get-tuple-element.15.qkv), custom_call_target="tpu_custom_call" | custom-call | flops 251658240 | bytes 2097152 | tf_op jit(solution)/shard_map/window_late/pallas_call | solution.py:143
  59.2 7.0 %collective-permute-done.5.halo = bf16[512,384]{1,0:T(8,128)(2,1)S(1)} collective-permute-done((bf16[512,384]{1,0:T(8,128)(2,1)S(1)}, bf16[512,384]{1,0:T(8,128)(2,1)S(1)}, u32[]{:S(2)}, u32[]{:S(2)}) %collective-permute-start.5) | collective-permute-done | bytes 393248 | tf_op jit(solution)/shard_map/ppermute | solution.py:536
  66.2 3.6 %window_early.1._ = bf16[1024,192]{1,0:T(8,128)(2,1)S(1)} custom-call(s32[9]{0:T(128)S(1)} %add_add_fusion.info, bf16[1024,576]{1,0:T(8,128)(2,1)S(1)} %get-tuple-element.15.qkv, bf16[512,384]{1,0:T(8,128)(2,1)S(1)} %collective-permute-done.5.halo, bf16[1024,192]{1,0:T(8,128)(2,1)S(1)} %window_late.1.before), custom_call_target="tpu_custom_call" | custom-call | flops 251658240 | bytes 2097152 | tf_op jit(solution)/shard_map/window_early/pallas_call | solution.py:143
  75.4 13.0 %collective-permute-done.6 = bf16[256,1536]{1,0:T(8,128)(2,1)S(1)} collective-permute-done((bf16[256,1536]{1,0:T(8,128)(2,1)S(1)}, bf16[256,1536]{1,0:T(8,128)(2,1)S(1)}, u32[]{:S(2)}, u32[]{:S(2)}) %collective-permute-start.6) | collective-permute-done | bytes 786464 | tf_op jit(solution)/shard_map/ppermute | solution.py:28
  89.4 3.8 %collective-permute-start.10 = (bf16[128,1536]{1,0:T(8,128)(2,1)S(1)}, bf16[128,1536]{1,0:T(8,128)(2,1)}, u32[]{:S(2)}, u32[]{:S(2)}) collective-permute-start(bf16[128,1536]{1,0:T(8,128)(2,1)S(1)} %get-tuple-element.37), channel_id=1, source_target_pairs={{0,3},{1,0},{2,1},{3,2},{4,7},{5,4},{6,5},{7,6},{8,11},{9,8},{10,9... | collective-permute-start | bytes 1179656 | tf_op jit(solution)/shard_map/ppermute | solution.py:28
  94.8 5.1 %collective-permute-done.10 = bf16[128,1536]{1,0:T(8,128)(2,1)} collective-permute-done((bf16[128,1536]{1,0:T(8,128)(2,1)S(1)}, bf16[128,1536]{1,0:T(8,128)(2,1)}, u32[]{:S(2)}, u32[]{:S(2)}) %collective-permute-start.10) | collective-permute-done | bytes 393248 | tf_op jit(solution)/shard_map/ppermute | solution.py:28
  101.4 3.8 %collective-permute-done.9 = bf16[128,1536]{1,0:T(8,128)(2,1)} collective-permute-done((bf16[128,1536]{1,0:T(8,128)(2,1)S(1)}, bf16[128,1536]{1,0:T(8,128)(2,1)}, u32[]{:S(2)}, u32[]{:S(2)}) %collective-permute-start.9) | collective-permute-done | bytes 393248 | tf_op jit(solution)/shard_map/ppermute | solution.py:28
  111.6 8.1 %collective-permute-done.12 = bf16[128,1536]{1,0:T(8,128)(2,1)S(1)} collective-permute-done((bf16[128,1536]{1,0:T(8,128)(2,1)S(1)}, bf16[128,1536]{1,0:T(8,128)(2,1)S(1)}, u32[]{:S(2)}, u32[]{:S(2)}) %collective-permute-start.12) | collective-permute-done | bytes 393248 | tf_op jit(solution)/shard_map/ppermute | solution.py:28
  119.6 5.5 %collective-permute-done.13 = bf16[128,1536]{1,0:T(8,128)(2,1)S(1)} collective-permute-done((bf16[128,1536]{1,0:T(8,128)(2,1)S(1)}, bf16[128,1536]{1,0:T(8,128)(2,1)S(1)}, u32[]{:S(2)}, u32[]{:S(2)}) %collective-permute-start.13) | collective-permute-done | bytes 393248 | tf_op jit(solution)/shard_map/ppermute | solution.py:28
  131.2 9.3 %collective-permute-done.20.refs_1_ = bf16[256,1536]{1,0:T(8,128)(2,1)S(1)} collective-permute-done((bf16[256,1536]{1,0:T(8,128)(2,1)S(1)}, bf16[256,1536]{1,0:T(8,128)(2,1)S(1)}, u32[]{:S(2)}, u32[]{:S(2)}) %collective-permute-start.20) | collective-permute-done | bytes 786464 | tf_op jit(solution)/shard_map/ppermute | solution.py:24
  150.5 9.4 %collective-permute-done.21 = bf16[128,1536]{1,0:T(8,128)(2,1)S(1)} collective-permute-done((bf16[128,1536]{1,0:T(8,128)(2,1)S(1)}, bf16[128,1536]{1,0:T(8,128)(2,1)S(1)}, u32[]{:S(2)}, u32[]{:S(2)}) %collective-permute-start.21) | collective-permute-done | bytes 393248 | tf_op jit(solution)/shard_map/ppermute | solution.py:28
  161.9 3.2 collective-permute-start.25
  168.8 3.3 collective-permute-done.25
  172.3 3.7 %collective-permute-start.27 = (bf16[64,1536]{1,0:T(8,128)(2,1)S(1)}, bf16[64,1536]{1,0:T(8,128)(2,1)S(1)}, u32[]{:S(2)}, u32[]{:S(2)}) collective-permute-start(bf16[64,1536]{1,0:T(8,128)(2,1)S(1)} %add_convert_fusion.10), channel_id=1, source_target_pairs={{0,3},{1,0},{2,1},{3,2},{4,7},{5,4},{6,5},{7,6},{8,11},{9,8},{10,9... | collective-permute-start | bytes 589832 | tf_op jit(solution)/shard_map/ppermute | solution.py:28
  179.2 3.7 %collective-permute-done.28 = bf16[64,1536]{1,0:T(8,128)(2,1)S(1)} collective-permute-done((bf16[64,1536]{1,0:T(8,128)(2,1)S(1)}, bf16[64,1536]{1,0:T(8,128)(2,1)S(1)}, u32[]{:S(2)}, u32[]{:S(2)}) %collective-permute-start.28) | collective-permute-done | bytes 196640 | tf_op jit(solution)/shard_map/ppermute | solution.py:28
  187.9 4.4 %collective-permute-done.30.diagonal = bf16[128,1536]{1,0:T(8,128)(2,1)S(1)} collective-permute-done((bf16[128,1536]{1,0:T(8,128)(2,1)}, bf16[128,1536]{1,0:T(8,128)(2,1)S(1)}, u32[]{:S(2)}, u32[]{:S(2)}) %collective-permute-start.30) | collective-permute-done | bytes 393248 | tf_op jit(solution)/shard_map/ppermute | solution.py:24
  198.3 18.2 %project_two.1 = (bf16[4,528,384]{2,1,0:T(8,128)(2,1)S(1)}, bf16[512,512]{1,0:T(8,128)(2,1)S(1)}) custom-call(s32[9]{0:T(128)S(1)} %concatenate.73.info, bf16[256,1536]{1,0:T(8,128)(2,1)S(1)} %pad_maximum_fusion.10.near, bf16[128,1536]{1,0:T(8,128)(2,1)S(1)} %copy-done.12, bf16[128,1536]{1,0:T(8,128)(2,1)S(1)} %copy-done.10, ...), custom_call_target="tpu_custom_call" | custom-call | flops 12884901888 | bytes 29360128 | tf_op jit(solution)/shard_map/project_two/pallas_call | solution.py:314
  219.8 5.6 %collective-permute-done.31 = bf16[528,384]{1,0:T(8,128)(2,1)S(1)} collective-permute-done((bf16[528,384]{1,0:T(8,128)(2,1)S(1)}, bf16[528,384]{1,0:T(8,128)(2,1)S(1)}, u32[]{:S(2)}, u32[]{:S(2)}) %collective-permute-start.31) | collective-permute-done | bytes 405536 | tf_op jit(solution)/shard_map/ppermute | solution.py:467
  227.2 4.2 %collective-permute-done.33 = bf16[528,384]{1,0:T(8,128)(2,1)S(1)} collective-permute-done((bf16[528,384]{1,0:T(8,128)(2,1)S(1)}, bf16[528,384]{1,0:T(8,128)(2,1)S(1)}, u32[]{:S(2)}, u32[]{:S(2)}) %collective-permute-start.33) | collective-permute-done | bytes 405536 | tf_op jit(solution)/shard_map/ppermute | solution.py:467
  236.5 12.3 %causal_own.1 = (f32[4,128,512]{2,1,0:T(8,128)S(1)}, f32[4,8,512]{2,1,0:T(8,128)S(1)}) custom-call(s32[3]{0:T(128)S(1)} %add_add_fusion.1.info, bf16[4,512,128]{2,1,0:T(8,128)(2,1)S(1)} %pad_maximum_fusion.11.queries, bf16[4,528,256]{2,1,0:T(8,128)(2,1)S(1)} %pad_maximum_fusion.2.kv, bf16[4,528,256]{2,1,0:T(8,128)(2,1)} %collective-permute-done.35.other), custom_call_target="tpu_custom_call" | custom-call | flops 2415919104 | bytes 4194304 | tf_op jit(solution)/shard_map/causal_own/pallas_call | solution.py:443
  248.8 12.6 %collective-permute-done.34 = bf16[4,528,256]{2,1,0:T(8,128)(2,1)} collective-permute-done((bf16[4,528,256]{2,1,0:T(8,128)(2,1)S(1)}, bf16[4,528,256]{2,1,0:T(8,128)(2,1)}, u32[]{:S(2)}, u32[]{:S(2)}) %collective-permute-start.34) | collective-permute-done | bytes 1081376 | tf_op jit(solution)/shard_map/ppermute | solution.py:589
  264.4 10.5 %causal_more.1 = (f32[4,128,512]{2,1,0:T(8,128)S(1)}, f32[4,8,512]{2,1,0:T(8,128)S(1)}) custom-call(s32[3]{0:T(128)S(1)} %add_add_fusion.1.info, bf16[4,512,128]{2,1,0:T(8,128)(2,1)S(1)} %pad_maximum_fusion.11.queries, bf16[4,528,256]{2,1,0:T(8,128)(2,1)} %broadcast_dynamic-update-slice_fusion.kv, f32[4,128,512]{2,1,0:T(8,128)S(1)} %get-tuple-element.22.rest_0_, ...), custom_call_target="tpu_custom_call" | custom-call | flops 2147483648 | bytes 4194304 | tf_op jit(solution)/shard_map/causal_more/pallas_call | solution.py:443
  274.9 9.6 %causal_last.1 = bf16[4,512,128]{2,1,0:T(8,128)(2,1)S(1)} custom-call(s32[3]{0:T(128)S(1)} %add_add_fusion.1.info, bf16[4,512,128]{2,1,0:T(8,128)(2,1)S(1)} %pad_maximum_fusion.11.queries, bf16[4,528,256]{2,1,0:T(8,128)(2,1)S(1)} %collective-permute-done.36.kv, f32[4,128,512]{2,1,0:T(8,128)S(1)} %get-tuple-element.23.start, ...), custom_call_target="tpu_custom_call" | custom-call | flops 2147483648 | bytes 4194304 | tf_op jit(solution)/shard_map/causal_last/pallas_call | solution.py:443
  296.7 3.2 collective-permute-start.45
  306.4 17.0 %collective-permute-done.45 = bf16[1024,512]{1,0:T(8,128)(2,1)S(1)} collective-permute-done((bf16[1024,512]{1,0:T(8,128)(2,1)S(1)}, bf16[1024,512]{1,0:T(8,128)(2,1)S(1)}, u32[]{:S(2)}, u32[]{:S(2)}) %collective-permute-start.45) | collective-permute-done | bytes 1048608 | tf_op jit(solution)/shard_map/ppermute | solution.py:28
  323.4 3.1 collective-permute-done.47
  332.4 7.3 %collective-permute-done.46 = bf16[512,512]{1,0:T(8,128)(2,1)S(1)} collective-permute-done((bf16[512,512]{1,0:T(8,128)(2,1)S(1)}, bf16[512,512]{1,0:T(8,128)(2,1)S(1)}, u32[]{:S(2)}, u32[]{:S(2)}) %collective-permute-start.46) | collective-permute-done | bytes 524320 | tf_op jit(solution)/shard_map/ppermute | solution.py:24
  (215 shorter events, 110.3 us)
Async XLA Ops:
  7.2 189.1 %all-gather.3.cloned.1.call-start = ((), (), s32[]{:S(2)}) async-start(), calls=%async_computation | async-start | bytes 14155776 | tf_op jit(solution)/shard_map/all_gather | solution.py:545
  9.2 13.9 %collective-permute-start = (bf16[128,1536]{1,0:T(8,128)(2,1)}, bf16[128,1536]{1,0:T(8,128)(2,1)S(1)}, u32[]{:S(2)}, u32[]{:S(2)}) collective-permute-start(bf16[128,1536]{1,0:T(8,128)(2,1)} %prepare.1), channel_id=1, source_target_pairs={{0,3},{1,0},{2,1},{3,2},{4,7},{5,4},{6,5},{7,6},{8,11},{9,8},{10,9... | collective-permute-start | bytes 1179656 | tf_op jit(solution)/shard_map/ppermute | solution.py:28
  13.3 15.6 %collective-permute-start.1 = (bf16[128,1536]{1,0:T(8,128)(2,1)}, bf16[128,1536]{1,0:T(8,128)(2,1)S(1)}, u32[]{:S(2)}, u32[]{:S(2)}) collective-permute-start(bf16[128,1536]{1,0:T(8,128)(2,1)} %prepare.1), channel_id=1, source_target_pairs={{0,4},{1,5},{2,6},{3,7},{4,0},{5,1},{6,2},{7,3},{8,12},{9,13},{10,... | collective-permute-start | bytes 1179656 | tf_op jit(solution)/shard_map/ppermute | solution.py:24
  14.1 13.5 %collective-permute-start.2 = (bf16[128,1536]{1,0:T(8,128)(2,1)}, bf16[128,1536]{1,0:T(8,128)(2,1)S(1)}, u32[]{:S(2)}, u32[]{:S(2)}) collective-permute-start(bf16[128,1536]{1,0:T(8,128)(2,1)} %prepare.1), channel_id=1, source_target_pairs={{0,1},{1,2},{2,3},{3,0},{4,5},{5,6},{6,7},{7,4},{8,9},{9,10},{10,1... | collective-permute-start | bytes 1179656 | tf_op jit(solution)/shard_map/ppermute | solution.py:28
  15.4 34.2 %collective-permute-start.15 = (bf16[208,512]{1,0:T(8,128)(2,1)S(1)}, bf16[208,512]{1,0:T(8,128)(2,1)S(1)}, u32[]{:S(2)}, u32[]{:S(2)}) collective-permute-start(bf16[208,512]{1,0:T(8,128)(2,1)S(1)} %pad_maximum_fusion.14), channel_id=1, source_target_pairs={{0,3},{1,0},{2,1},{3,2},{4,7},{5,4},{6,5},{7,6},{8,11},{9,8},{10,9... | collective-permute-start | bytes 638984 | tf_op jit(solution)/shard_map/ppermute | solution.py:28
  18.6 31.0 %collective-permute-start.16 = (bf16[208,512]{1,0:T(8,128)(2,1)S(1)}, bf16[208,512]{1,0:T(8,128)(2,1)}, u32[]{:S(2)}, u32[]{:S(2)}) collective-permute-start(bf16[208,512]{1,0:T(8,128)(2,1)S(1)} %pad_maximum_fusion.14), channel_id=1, source_target_pairs={{0,1},{1,2},{2,3},{3,0},{4,5},{5,6},{6,7},{7,4},{8,9},{9,10},{10,1... | collective-permute-start | bytes 638984 | tf_op jit(solution)/shard_map/ppermute | solution.py:28
  23.1 28.4 %collective-permute-start.14 = (bf16[208,512]{1,0:T(8,128)(2,1)S(1)}, bf16[208,512]{1,0:T(8,128)(2,1)S(1)}, u32[]{:S(2)}, u32[]{:S(2)}) collective-permute-start(bf16[208,512]{1,0:T(8,128)(2,1)S(1)} %pad_maximum_fusion.14), channel_id=1, source_target_pairs={{0,4},{1,5},{2,6},{3,7},{4,0},{5,1},{6,2},{7,3},{8,12},{9,13},{10,... | collective-permute-start | bytes 638984 | tf_op jit(solution)/shard_map/ppermute | solution.py:24
  27.6 18.2 %collective-permute-start.4 = (bf16[256,1536]{1,0:T(8,128)(2,1)S(1)}, bf16[256,1536]{1,0:T(8,128)(2,1)S(1)}, u32[]{:S(2)}, u32[]{:S(2)}) collective-permute-start(bf16[256,1536]{1,0:T(8,128)(2,1)S(1)} %pad_maximum_fusion.7), channel_id=1, source_target_pairs={{0,4},{1,5},{2,6},{3,7},{4,0},{5,1},{6,2},{7,3},{8,12},{9,13},{10,... | collective-permute-start | bytes 2359304 | tf_op jit(solution)/shard_map/ppermute | solution.py:24
  29.0 17.4 %collective-permute-start.3 = (bf16[256,1536]{1,0:T(8,128)(2,1)S(1)}, bf16[256,1536]{1,0:T(8,128)(2,1)S(1)}, u32[]{:S(2)}, u32[]{:S(2)}) collective-permute-start(bf16[256,1536]{1,0:T(8,128)(2,1)S(1)} %pad_maximum_fusion.6), channel_id=1, source_target_pairs={{0,2},{1,3},{2,0},{3,1},{4,6},{5,7},{6,4},{7,5},{8,10},{9,11},{10,... | collective-permute-start | bytes 2359304 | tf_op jit(solution)/shard_map/ppermute | solution.py:28
  50.6 19.2 %collective-permute-start.18 = (bf16[416,512]{1,0:T(8,128)(2,1)S(1)}, bf16[416,512]{1,0:T(8,128)(2,1)S(1)}, u32[]{:S(2)}, u32[]{:S(2)}) collective-permute-start(bf16[416,512]{1,0:T(8,128)(2,1)S(1)} %maximum_add_fusion.1), channel_id=1, source_target_pairs={{0,4},{1,5},{2,6},{3,7},{4,0},{5,1},{6,2},{7,3},{8,12},{9,13},{10,... | collective-permute-start | bytes 1277960 | tf_op jit(solution)/shard_map/ppermute | solution.py:24
  51.6 18.2 %collective-permute-start.17 = (bf16[416,512]{1,0:T(8,128)(2,1)S(1)}, bf16[416,512]{1,0:T(8,128)(2,1)S(1)}, u32[]{:S(2)}, u32[]{:S(2)}) collective-permute-start(bf16[416,512]{1,0:T(8,128)(2,1)S(1)} %maximum_add_fusion), channel_id=1, source_target_pairs={{0,2},{1,3},{2,0},{3,1},{4,6},{5,7},{6,4},{7,5},{8,10},{9,11},{10,... | collective-permute-start | bytes 1277960 | tf_op jit(solution)/shard_map/ppermute | solution.py:28
  53.5 12.7 %collective-permute-start.5 = (bf16[512,384]{1,0:T(8,128)(2,1)S(1)}, bf16[512,384]{1,0:T(8,128)(2,1)S(1)}, u32[]{:S(2)}, u32[]{:S(2)}) collective-permute-start(bf16[512,384]{1,0:T(8,128)(2,1)S(1)} %get-tuple-element.16), channel_id=1, source_target_pairs={{0,8},{8,16},{16,24},{24,32},{32,40},{40,48},{48,56},{56,64},{64,7... | collective-permute-start | bytes 1179656 | tf_op jit(solution)/shard_map/ppermute | solution.py:536
  71.8 16.6 %collective-permute-start.6 = (bf16[256,1536]{1,0:T(8,128)(2,1)S(1)}, bf16[256,1536]{1,0:T(8,128)(2,1)S(1)}, u32[]{:S(2)}, u32[]{:S(2)}) collective-permute-start(bf16[256,1536]{1,0:T(8,128)(2,1)S(1)} %get-tuple-element.53), channel_id=1, source_target_pairs={{0,2},{1,3},{2,0},{3,1},{4,6},{5,7},{6,4},{7,5},{8,10},{9,11},{10,... | collective-permute-start | bytes 2359304 | tf_op jit(solution)/shard_map/ppermute | solution.py:28
  74.4 14.7 %collective-permute-start.8 = (bf16[256,1536]{1,0:T(8,128)(2,1)S(1)}, bf16[256,1536]{1,0:T(8,128)(2,1)S(1)}, u32[]{:S(2)}, u32[]{:S(2)}) collective-permute-start(bf16[256,1536]{1,0:T(8,128)(2,1)S(1)} %get-tuple-element.54), channel_id=1, source_target_pairs={{0,4},{1,5},{2,6},{3,7},{4,0},{5,1},{6,2},{7,3},{8,12},{9,13},{10,... | collective-permute-start | bytes 2359304 | tf_op jit(solution)/shard_map/ppermute | solution.py:24
  107.5 12.1 %collective-permute-start.12 = (bf16[128,1536]{1,0:T(8,128)(2,1)S(1)}, bf16[128,1536]{1,0:T(8,128)(2,1)S(1)}, u32[]{:S(2)}, u32[]{:S(2)}) collective-permute-start(bf16[128,1536]{1,0:T(8,128)(2,1)S(1)} %fusion.7), channel_id=1, source_target_pairs={{0,3},{1,0},{2,1},{3,2},{4,7},{5,4},{6,5},{7,6},{8,11},{9,8},{10,9... | collective-permute-start | bytes 1179656 | tf_op jit(solution)/shard_map/ppermute | solution.py:28
  107.6 17.5 %collective-permute-start.13 = (bf16[128,1536]{1,0:T(8,128)(2,1)S(1)}, bf16[128,1536]{1,0:T(8,128)(2,1)S(1)}, u32[]{:S(2)}, u32[]{:S(2)}) collective-permute-start(bf16[128,1536]{1,0:T(8,128)(2,1)S(1)} %fusion.7), channel_id=1, source_target_pairs={{0,1},{1,2},{2,3},{3,0},{4,5},{5,6},{6,7},{7,4},{8,9},{9,10},{10,1... | collective-permute-start | bytes 1179656 | tf_op jit(solution)/shard_map/ppermute | solution.py:28
  109.9 15.3 %collective-permute-start.11 = (bf16[128,1536]{1,0:T(8,128)(2,1)S(1)}, bf16[128,1536]{1,0:T(8,128)(2,1)S(1)}, u32[]{:S(2)}, u32[]{:S(2)}) collective-permute-start(bf16[128,1536]{1,0:T(8,128)(2,1)S(1)} %fusion.7), channel_id=1, source_target_pairs={{0,4},{1,5},{2,6},{3,7},{4,0},{5,1},{6,2},{7,3},{8,12},{9,13},{10,... | collective-permute-start | bytes 1179656 | tf_op jit(solution)/shard_map/ppermute | solution.py:24
  125.1 15.3 %collective-permute-start.20 = (bf16[256,1536]{1,0:T(8,128)(2,1)S(1)}, bf16[256,1536]{1,0:T(8,128)(2,1)S(1)}, u32[]{:S(2)}, u32[]{:S(2)}) collective-permute-start(bf16[256,1536]{1,0:T(8,128)(2,1)S(1)} %pad_maximum_fusion.9), channel_id=1, source_target_pairs={{0,4},{1,5},{2,6},{3,7},{4,0},{5,1},{6,2},{7,3},{8,12},{9,13},{10,... | collective-permute-start | bytes 2359304 | tf_op jit(solution)/shard_map/ppermute | solution.py:24
  125.3 18.0 %collective-permute-start.19 = (bf16[256,1536]{1,0:T(8,128)(2,1)S(1)}, bf16[256,1536]{1,0:T(8,128)(2,1)S(1)}, u32[]{:S(2)}, u32[]{:S(2)}) collective-permute-start(bf16[256,1536]{1,0:T(8,128)(2,1)S(1)} %pad_maximum_fusion.8), channel_id=1, source_target_pairs={{0,2},{1,3},{2,0},{3,1},{4,6},{5,7},{6,4},{7,5},{8,10},{9,11},{10,... | collective-permute-start | bytes 2359304 | tf_op jit(solution)/shard_map/ppermute | solution.py:28
  148.3 11.6 %collective-permute-start.21 = (bf16[128,1536]{1,0:T(8,128)(2,1)S(1)}, bf16[128,1536]{1,0:T(8,128)(2,1)S(1)}, u32[]{:S(2)}, u32[]{:S(2)}) collective-permute-start(bf16[128,1536]{1,0:T(8,128)(2,1)S(1)} %get-tuple-element.50), channel_id=1, source_target_pairs={{0,2},{1,3},{2,0},{3,1},{4,6},{5,7},{6,4},{7,5},{8,10},{9,11},{10,... | collective-permute-start | bytes 1179656 | tf_op jit(solution)/shard_map/ppermute | solution.py:28
  148.4 11.5 %collective-permute-start.23 = (bf16[128,1536]{1,0:T(8,128)(2,1)S(1)}, bf16[128,1536]{1,0:T(8,128)(2,1)S(1)}, u32[]{:S(2)}, u32[]{:S(2)}) collective-permute-start(bf16[128,1536]{1,0:T(8,128)(2,1)S(1)} %get-tuple-element.51), channel_id=1, source_target_pairs={{0,4},{1,5},{2,6},{3,7},{4,0},{5,1},{6,2},{7,3},{8,12},{9,13},{10,... | collective-permute-start | bytes 1179656 | tf_op jit(solution)/shard_map/ppermute | solution.py:24
  217.7 13.7 %collective-permute-start.33 = (bf16[528,384]{1,0:T(8,128)(2,1)S(1)}, bf16[528,384]{1,0:T(8,128)(2,1)S(1)}, u32[]{:S(2)}, u32[]{:S(2)}) collective-permute-start(bf16[528,384]{1,0:T(8,128)(2,1)S(1)} %get-tuple-element.43), channel_id=1, source_target_pairs={{0,16},{8,24},{16,32},{24,40},{32,48},{40,56},{48,0},{56,8},{64,80... | collective-permute-start | bytes 1216520 | tf_op jit(solution)/shard_map/ppermute | solution.py:467
  232.2 29.2 %collective-permute-start.34 = (bf16[4,528,256]{2,1,0:T(8,128)(2,1)S(1)}, bf16[4,528,256]{2,1,0:T(8,128)(2,1)}, u32[]{:S(2)}, u32[]{:S(2)}) collective-permute-start(bf16[4,528,256]{2,1,0:T(8,128)(2,1)S(1)} %pad_maximum_fusion.2.kv), channel_id=1, source_target_pairs={{0,64},{8,72},{16,80},{24,88},{32,96},{40,104},{48,112},{56,120},{... | collective-permute-start | bytes 3244040 | tf_op jit(solution)/shard_map/ppermute | solution.py:589
  262.0 12.9 %collective-permute-start.36 = (bf16[4,528,256]{2,1,0:T(8,128)(2,1)}, bf16[4,528,256]{2,1,0:T(8,128)(2,1)S(1)}, u32[]{:S(2)}, u32[]{:S(2)}) collective-permute-start(bf16[4,528,256]{2,1,0:T(8,128)(2,1)} %broadcast_dynamic-update-slice_fusion.kv), channel_id=1, source_target_pairs={{0,8},{8,0},{16,24},{24,16},{32,40},{40,32},{48,56},{56,48},{64,72... | collective-permute-start | bytes 3244040 | tf_op jit(solution)/shard_map/ppermute | solution.py:508
  262.2 25.7 %collective-permute-start.37 = (bf16[256,1536]{1,0:T(8,128)(2,1)S(1)}, bf16[256,1536]{1,0:T(8,128)(2,1)S(1)}, u32[]{:S(2)}, u32[]{:S(2)}) collective-permute-start(bf16[256,1536]{1,0:T(8,128)(2,1)S(1)} %get-tuple-element.47), channel_id=1, source_target_pairs={{0,2},{1,3},{2,0},{3,1},{4,6},{5,7},{6,4},{7,5},{8,10},{9,11},{10,... | collective-permute-start | bytes 2359304 | tf_op jit(solution)/shard_map/ppermute | solution.py:28
  262.3 25.7 %collective-permute-start.39 = (bf16[256,1536]{1,0:T(8,128)(2,1)S(1)}, bf16[256,1536]{1,0:T(8,128)(2,1)S(1)}, u32[]{:S(2)}, u32[]{:S(2)}) collective-permute-start(bf16[256,1536]{1,0:T(8,128)(2,1)S(1)} %get-tuple-element.48), channel_id=1, source_target_pairs={{0,4},{1,5},{2,6},{3,7},{4,0},{5,1},{6,2},{7,3},{8,12},{9,13},{10,... | collective-permute-start | bytes 2359304 | tf_op jit(solution)/shard_map/ppermute | solution.py:24
  288.3 13.7 %collective-permute-start.38 = (bf16[128,1536]{1,0:T(8,128)(2,1)S(1)}, bf16[128,1536]{1,0:T(8,128)(2,1)S(1)}, u32[]{:S(2)}, u32[]{:S(2)}) collective-permute-start(bf16[128,1536]{1,0:T(8,128)(2,1)S(1)} %get-tuple-element.46), channel_id=1, source_target_pairs={{0,4},{1,5},{2,6},{3,7},{4,0},{5,1},{6,2},{7,3},{8,12},{9,13},{10,... | collective-permute-start | bytes 1179656 | tf_op jit(solution)/shard_map/ppermute | solution.py:24
  288.5 13.5 %collective-permute-start.40 = (bf16[128,1536]{1,0:T(8,128)(2,1)S(1)}, bf16[128,1536]{1,0:T(8,128)(2,1)S(1)}, u32[]{:S(2)}, u32[]{:S(2)}) collective-permute-start(bf16[128,1536]{1,0:T(8,128)(2,1)S(1)} %get-tuple-element.34), channel_id=1, source_target_pairs={{0,1},{1,2},{2,3},{3,0},{4,5},{5,6},{6,7},{7,4},{8,9},{9,10},{10,1... | collective-permute-start | bytes 1179656 | tf_op jit(solution)/shard_map/ppermute | solution.py:28
  296.7 26.7 %collective-permute-start.45 = (bf16[1024,512]{1,0:T(8,128)(2,1)S(1)}, bf16[1024,512]{1,0:T(8,128)(2,1)S(1)}, u32[]{:S(2)}, u32[]{:S(2)}) collective-permute-start(bf16[1024,512]{1,0:T(8,128)(2,1)S(1)} %output_columns.4), channel_id=1, source_target_pairs={{0,2},{1,3},{2,0},{3,1},{4,6},{5,7},{6,4},{7,5},{8,10},{9,11},{10,... | collective-permute-start | bytes 3145736 | tf_op jit(solution)/shard_map/ppermute | solution.py:28
  301.6 24.9 %collective-permute-start.47 = (bf16[1024,512]{1,0:T(8,128)(2,1)S(1)}, bf16[1024,512]{1,0:T(8,128)(2,1)S(1)}, u32[]{:S(2)}, u32[]{:S(2)}) collective-permute-start(bf16[1024,512]{1,0:T(8,128)(2,1)S(1)} %output_columns.5), channel_id=1, source_target_pairs={{0,4},{1,5},{2,6},{3,7},{4,0},{5,1},{6,2},{7,3},{8,12},{9,13},{10,... | collective-permute-start | bytes 3145736 | tf_op jit(solution)/shard_map/ppermute | solution.py:24
  327.0 12.8 %collective-permute-start.46 = (bf16[512,512]{1,0:T(8,128)(2,1)S(1)}, bf16[512,512]{1,0:T(8,128)(2,1)S(1)}, u32[]{:S(2)}, u32[]{:S(2)}) collective-permute-start(bf16[512,512]{1,0:T(8,128)(2,1)S(1)} %get-tuple-element.38), channel_id=1, source_target_pairs={{0,4},{1,5},{2,6},{3,7},{4,0},{5,1},{6,2},{7,3},{8,12},{9,13},{10,... | collective-permute-start | bytes 1572872 | tf_op jit(solution)/shard_map/ppermute | solution.py:24
  328.7 12.3 %collective-permute-start.48 = (bf16[512,512]{1,0:T(8,128)(2,1)S(1)}, bf16[512,512]{1,0:T(8,128)(2,1)S(1)}, u32[]{:S(2)}, u32[]{:S(2)}) collective-permute-start(bf16[512,512]{1,0:T(8,128)(2,1)S(1)} %get-tuple-element.30), channel_id=1, source_target_pairs={{0,1},{1,2},{2,3},{3,0},{4,5},{5,6},{6,7},{7,4},{8,9},{9,10},{10,1... | collective-permute-start | bytes 1572872 | tf_op jit(solution)/shard_map/ppermute | solution.py:28
  (49 other events, 364.9 us)
Sparse Core Ops, SparseCore 0:
  71.3 65.1 all-gather.2

commit v2 on v0

--- a/solution.py
+++ b/solution.py
@@ -585,16 +585,19 @@
     first_kv = lax.ppermute(own_kv, "seq", [(i, i + 8) for i in range(8)])
     info_two = jnp.stack([half, core, y]).astype(jnp.int32)
     running = causal_attend(True, info_two, queries, (own_kv, flip_seq(own_kv, 1)))
-    first_kv = first_kv + running[1][0, 2, 0].astype(BF16)
+    unread = jnp.broadcast_to(running[1][0:1, 2:3, :128], (1, EXT, 128)).astype(BF16)
+    first_kv = lax.dynamic_update_slice(first_kv, unread, (0, capacity, 128))
     mixed = causal_attend(False, info_two, queries, (first_kv, flip_seq(first_kv, 1)), running)
     back = [mixed[0], turn_y(mixed[3], 3), turn_y(mixed[2], 2), turn_y(mixed[1], 1)]
     out_opposite = turn_z(output_columns(block_of[4:6], y, back, heads_out_two), 2)
-    out_diagonal = flip_x(output_columns(block_of[6:], y, back, heads_out_two))
+    out_diagonal = output_columns(block_of[6:], y, back, heads_out_two)
+    after_out = out_diagonal
+    out_diagonal = flip_x(out_diagonal)
     level_one = (
         mid_stream.astype(F32)
-        + reduce_second(later(mlp_near, mixed[0]), opposite, diagonal)
+        + reduce_second(later(mlp_near, after_out), opposite, diagonal)
     ).astype(BF16)
-    out_near = output_columns(later(block_of[:4], level_one), y, back, heads_out_two)
+    out_near = output_columns(block_of[:4], y, back, heads_out_two)
     level_two = (
         (wide_cols.astype(F32) + reduce_second(out_near, out_opposite, out_diagonal)) * validity[:, None]
     ).astype(BF16)

time: 354 us -> 363 us (1.025)
  waiting for transfers between devices: 163 us -> 167 us
    ppermute x6, waiting for transfers between devices: 13.8 us -> 20.1 us  [turn_y(): lax.ppermute(value, 'seq', [(i, i & 9 | i + 2 * steps & 6) for i in range...]
  transfers between devices with their start and end apart: 51 -> 51, of which waited for: 32 -> 34; matrix products, arithmetic and copies ran while one was open for 6% -> 7% of each run, Pallas kernels for 15% -> 15%
where the time goes in v2:
time: 363 us; the launch traced here: 357 us
  waiting for transfers between devices  167 us (46%)
  Pallas kernels  73.7 us (20%)
  starting transfers between devices  56.8 us (16%)
  local copies, waits for them, and re-layouts  19.8 us (5%)
  between operations  19.1 us (5%)
  other arithmetic  16.3 us (4%)
  matrix products  3.73 us (1%)
    ppermute x24, waiting for transfers between devices, turn_z(): lax.ppermute(value, 'blk', [(i, i & 4 | i + steps & 3) for i in range(8)])  94.3 us
    ppermute x16, waiting for transfers between devices, flip_x(): return lax.ppermute(value, 'blk', [(i, i ^ 4) for i in range(8)])  33.5 us
    ppermute x24, starting transfers between devices, turn_z(): lax.ppermute(value, 'blk', [(i, i & 4 | i + steps & 3) for i in range(8)])  32.3 us
    pallas_call x2, Pallas kernels, causal_attend(): pl.pallas_call(kernel, out_shape=out_shape, grid_spec=pltpu.PrefetchScala...  30.1 us
    ppermute x6, waiting for transfers between devices, turn_y(): lax.ppermute(value, 'seq', [(i, i & 9 | i + 2 * steps & 6) for i in range...  20.1 us
    pallas_call x1, Pallas kernels, project_two(): pl.pallas_call(project_kernel, out_shape=(jax.ShapeDtypeStruct((4, 512 +...  18.2 us
    ppermute x16, starting transfers between devices, flip_x(): return lax.ppermute(value, 'blk', [(i, i ^ 4) for i in range(8)])  16.7 us
    ppermute x1, waiting for transfers between devices, per_device(): first_kv = lax.ppermute(own_kv, 'seq', [(i, i + 8) for i in range(8)])  12.5 us
  transfers between devices with their start and end apart: 51, of which 34 were waited for; matrix products, arithmetic and copies ran while one was open for 7% of the time, Pallas kernels for 15%

profile of v2, /device:TPU:6, one launch (start us, length us, event | category | flops | bytes accessed | tf_op | source)
XLA Modules:
  0.0 356.8 jit_solution(5164966500638212385)
XLA Ops:
  9.2 4.0 %collective-permute-start = (bf16[128,1536]{1,0:T(8,128)(2,1)}, bf16[128,1536]{1,0:T(8,128)(2,1)S(1)}, u32[]{:S(2)}, u32[]{:S(2)}) collective-permute-start(bf16[128,1536]{1,0:T(8,128)(2,1)} %prepare.1), channel_id=1, source_target_pairs={{0,3},{1,0},{2,1},{3,2},{4,7},{5,4},{6,5},{7,6},{8,11},{9,8},{10,9... | collective-permute-start | bytes 1179656 | tf_op jit(solution)/shard_map/ppermute | solution.py:28
  15.4 3.2 collective-permute-start.15
  18.8 4.3 %collective-permute-done = bf16[128,1536]{1,0:T(8,128)(2,1)S(1)} collective-permute-done((bf16[128,1536]{1,0:T(8,128)(2,1)}, bf16[128,1536]{1,0:T(8,128)(2,1)S(1)}, u32[]{:S(2)}, u32[]{:S(2)}) %collective-permute-start) | collective-permute-done | bytes 393248 | tf_op jit(solution)/shard_map/ppermute | solution.py:28
  23.9 3.6 %collective-permute-done.2 = bf16[128,1536]{1,0:T(8,128)(2,1)S(1)} collective-permute-done((bf16[128,1536]{1,0:T(8,128)(2,1)}, bf16[128,1536]{1,0:T(8,128)(2,1)S(1)}, u32[]{:S(2)}, u32[]{:S(2)}) %collective-permute-start.2) | collective-permute-done | bytes 393248 | tf_op jit(solution)/shard_map/ppermute | solution.py:28
  35.5 10.3 %collective-permute-done.4.diagonal = bf16[256,1536]{1,0:T(8,128)(2,1)S(1)} collective-permute-done((bf16[256,1536]{1,0:T(8,128)(2,1)S(1)}, bf16[256,1536]{1,0:T(8,128)(2,1)S(1)}, u32[]{:S(2)}, u32[]{:S(2)}) %collective-permute-start.4) | collective-permute-done | bytes 786464 | tf_op jit(solution)/shard_map/ppermute | solution.py:24
  55.6 3.5 window_late.1.before
  59.2 7.0 %collective-permute-done.5.halo = bf16[512,384]{1,0:T(8,128)(2,1)S(1)} collective-permute-done((bf16[512,384]{1,0:T(8,128)(2,1)S(1)}, bf16[512,384]{1,0:T(8,128)(2,1)S(1)}, u32[]{:S(2)}, u32[]{:S(2)}) %collective-permute-start.5) | collective-permute-done | bytes 393248 | tf_op jit(solution)/shard_map/ppermute | solution.py:532
  66.2 3.6 %window_early.1._ = bf16[1024,192]{1,0:T(8,128)(2,1)S(1)} custom-call(s32[9]{0:T(128)S(1)} %add_add_fusion.info, bf16[1024,576]{1,0:T(8,128)(2,1)S(1)} %get-tuple-element.13.qkv, bf16[512,384]{1,0:T(8,128)(2,1)S(1)} %collective-permute-done.5.halo, bf16[1024,192]{1,0:T(8,128)(2,1)S(1)} %window_late.1.before), custom_call_target="tpu_custom_call" | custom-call | flops 251658240 | bytes 2097152 | tf_op jit(solution)/shard_map/window_early/pallas_call | solution.py:143
  75.4 13.0 %collective-permute-done.6 = bf16[256,1536]{1,0:T(8,128)(2,1)S(1)} collective-permute-done((bf16[256,1536]{1,0:T(8,128)(2,1)S(1)}, bf16[256,1536]{1,0:T(8,128)(2,1)S(1)}, u32[]{:S(2)}, u32[]{:S(2)}) %collective-permute-start.6) | collective-permute-done | bytes 786464 | tf_op jit(solution)/shard_map/ppermute | solution.py:28
  89.5 3.8 %collective-permute-start.10 = (bf16[128,1536]{1,0:T(8,128)(2,1)S(1)}, bf16[128,1536]{1,0:T(8,128)(2,1)}, u32[]{:S(2)}, u32[]{:S(2)}) collective-permute-start(bf16[128,1536]{1,0:T(8,128)(2,1)S(1)} %get-tuple-element.33), channel_id=1, source_target_pairs={{0,3},{1,0},{2,1},{3,2},{4,7},{5,4},{6,5},{7,6},{8,11},{9,8},{10,9... | collective-permute-start | bytes 1179656 | tf_op jit(solution)/shard_map/ppermute | solution.py:28
  94.8 5.1 %collective-permute-done.10 = bf16[128,1536]{1,0:T(8,128)(2,1)} collective-permute-done((bf16[128,1536]{1,0:T(8,128)(2,1)S(1)}, bf16[128,1536]{1,0:T(8,128)(2,1)}, u32[]{:S(2)}, u32[]{:S(2)}) %collective-permute-start.10) | collective-permute-done | bytes 393248 | tf_op jit(solution)/shard_map/ppermute | solution.py:28
  101.4 3.9 %collective-permute-done.9 = bf16[128,1536]{1,0:T(8,128)(2,1)} collective-permute-done((bf16[128,1536]{1,0:T(8,128)(2,1)S(1)}, bf16[128,1536]{1,0:T(8,128)(2,1)}, u32[]{:S(2)}, u32[]{:S(2)}) %collective-permute-start.9) | collective-permute-done | bytes 393248 | tf_op jit(solution)/shard_map/ppermute | solution.py:28
  111.6 8.1 %collective-permute-done.12 = bf16[128,1536]{1,0:T(8,128)(2,1)S(1)} collective-permute-done((bf16[128,1536]{1,0:T(8,128)(2,1)S(1)}, bf16[128,1536]{1,0:T(8,128)(2,1)S(1)}, u32[]{:S(2)}, u32[]{:S(2)}) %collective-permute-start.12) | collective-permute-done | bytes 393248 | tf_op jit(solution)/shard_map/ppermute | solution.py:28
  119.7 5.5 %collective-permute-done.13 = bf16[128,1536]{1,0:T(8,128)(2,1)S(1)} collective-permute-done((bf16[128,1536]{1,0:T(8,128)(2,1)S(1)}, bf16[128,1536]{1,0:T(8,128)(2,1)S(1)}, u32[]{:S(2)}, u32[]{:S(2)}) %collective-permute-start.13) | collective-permute-done | bytes 393248 | tf_op jit(solution)/shard_map/ppermute | solution.py:28
  131.2 9.3 %collective-permute-done.20.refs_1_ = bf16[256,1536]{1,0:T(8,128)(2,1)S(1)} collective-permute-done((bf16[256,1536]{1,0:T(8,128)(2,1)S(1)}, bf16[256,1536]{1,0:T(8,128)(2,1)S(1)}, u32[]{:S(2)}, u32[]{:S(2)}) %collective-permute-start.20) | collective-permute-done | bytes 786464 | tf_op jit(solution)/shard_map/ppermute | solution.py:24
  150.5 9.4 %collective-permute-done.21 = bf16[128,1536]{1,0:T(8,128)(2,1)S(1)} collective-permute-done((bf16[128,1536]{1,0:T(8,128)(2,1)S(1)}, bf16[128,1536]{1,0:T(8,128)(2,1)S(1)}, u32[]{:S(2)}, u32[]{:S(2)}) %collective-permute-start.21) | collective-permute-done | bytes 393248 | tf_op jit(solution)/shard_map/ppermute | solution.py:28
  161.9 3.2 collective-permute-start.25
  168.8 3.3 collective-permute-done.25
  172.3 3.7 %collective-permute-start.27 = (bf16[64,1536]{1,0:T(8,128)(2,1)S(1)}, bf16[64,1536]{1,0:T(8,128)(2,1)S(1)}, u32[]{:S(2)}, u32[]{:S(2)}) collective-permute-start(bf16[64,1536]{1,0:T(8,128)(2,1)S(1)} %add_convert_fusion.10), channel_id=1, source_target_pairs={{0,3},{1,0},{2,1},{3,2},{4,7},{5,4},{6,5},{7,6},{8,11},{9,8},{10,9... | collective-permute-start | bytes 589832 | tf_op jit(solution)/shard_map/ppermute | solution.py:28
  179.2 3.7 %collective-permute-done.28 = bf16[64,1536]{1,0:T(8,128)(2,1)S(1)} collective-permute-done((bf16[64,1536]{1,0:T(8,128)(2,1)S(1)}, bf16[64,1536]{1,0:T(8,128)(2,1)S(1)}, u32[]{:S(2)}, u32[]{:S(2)}) %collective-permute-start.28) | collective-permute-done | bytes 196640 | tf_op jit(solution)/shard_map/ppermute | solution.py:28
  187.9 4.5 %collective-permute-done.30.diagonal = bf16[128,1536]{1,0:T(8,128)(2,1)S(1)} collective-permute-done((bf16[128,1536]{1,0:T(8,128)(2,1)}, bf16[128,1536]{1,0:T(8,128)(2,1)S(1)}, u32[]{:S(2)}, u32[]{:S(2)}) %collective-permute-start.30) | collective-permute-done | bytes 393248 | tf_op jit(solution)/shard_map/ppermute | solution.py:24
  198.3 18.2 %project_two.1 = (bf16[4,528,384]{2,1,0:T(8,128)(2,1)S(1)}, bf16[512,512]{1,0:T(8,128)(2,1)S(1)}) custom-call(s32[9]{0:T(128)S(1)} %concatenate.75.info, bf16[256,1536]{1,0:T(8,128)(2,1)S(1)} %pad_maximum_fusion.10.near, bf16[128,1536]{1,0:T(8,128)(2,1)S(1)} %copy-done.13, bf16[128,1536]{1,0:T(8,128)(2,1)S(1)} %copy-done.11, ...), custom_call_target="tpu_custom_call" | custom-call | flops 12884901888 | bytes 29360128 | tf_op jit(solution)/shard_map/project_two/pallas_call | solution.py:314
  219.8 5.6 %collective-permute-done.31 = bf16[528,384]{1,0:T(8,128)(2,1)S(1)} collective-permute-done((bf16[528,384]{1,0:T(8,128)(2,1)S(1)}, bf16[528,384]{1,0:T(8,128)(2,1)S(1)}, u32[]{:S(2)}, u32[]{:S(2)}) %collective-permute-start.31) | collective-permute-done | bytes 405536 | tf_op jit(solution)/shard_map/ppermute | solution.py:463
  227.3 4.2 %collective-permute-done.33 = bf16[528,384]{1,0:T(8,128)(2,1)S(1)} collective-permute-done((bf16[528,384]{1,0:T(8,128)(2,1)S(1)}, bf16[528,384]{1,0:T(8,128)(2,1)S(1)}, u32[]{:S(2)}, u32[]{:S(2)}) %collective-permute-start.33) | collective-permute-done | bytes 405536 | tf_op jit(solution)/shard_map/ppermute | solution.py:463
  236.7 12.3 %causal_own.1 = (f32[4,128,512]{2,1,0:T(8,128)S(1)}, f32[4,8,512]{2,1,0:T(8,128)S(1)}) custom-call(s32[3]{0:T(128)S(1)} %add_add_fusion.2.info, bf16[4,512,128]{2,1,0:T(8,128)(2,1)S(1)} %pad_maximum_fusion.11.queries, bf16[4,528,256]{2,1,0:T(8,128)(2,1)S(1)} %pad_maximum_fusion.2.kv, bf16[4,528,256]{2,1,0:T(8,128)(2,1)} %collective-permute-done.35.other), custom_call_target="tpu_custom_call" | custom-call | flops 2415919104 | bytes 4194304 | tf_op jit(solution)/shard_map/causal_own/pallas_call | solution.py:439
  249.0 12.5 %collective-permute-done.34 = bf16[4,528,256]{2,1,0:T(8,128)(2,1)} collective-permute-done((bf16[4,528,256]{2,1,0:T(8,128)(2,1)S(1)}, bf16[4,528,256]{2,1,0:T(8,128)(2,1)}, u32[]{:S(2)}, u32[]{:S(2)}) %collective-permute-start.34) | collective-permute-done | bytes 1081376 | tf_op jit(solution)/shard_map/ppermute | solution.py:585
  265.4 17.8 %causal_first_half.1 = bf16[4,512,128]{2,1,0:T(8,128)(2,1)S(1)} custom-call(s32[3]{0:T(128)S(1)} %add_add_fusion.2.info, bf16[4,512,128]{2,1,0:T(8,128)(2,1)S(1)} %pad_maximum_fusion.11.queries, bf16[4,528,256]{2,1,0:T(8,128)(2,1)} %broadcast_dynamic-update-slice_fusion.kv, bf16[4,528,256]{2,1,0:T(8,128)(2,1)S(1)} %collective-permute-done.36.other, ...), custom_call_target="tpu_custom_call" | custom-call | flops 4294967296 | bytes 4194304 | tf_op jit(solution)/shard_map/causal_first_half/pallas_call | solution.py:439
  286.1 4.3 %collective-permute-done.37.refs_2_ = bf16[512,128]{1,0:T(8,128)(2,1)S(1)} collective-permute-done((bf16[512,128]{1,0:T(8,128)(2,1)}, bf16[512,128]{1,0:T(8,128)(2,1)S(1)}, u32[]{:S(2)}, u32[]{:S(2)}) %collective-permute-start.37) | collective-permute-done | bytes 131104 | tf_op jit(solution)/shard_map/ppermute | solution.py:463
  308.1 3.2 collective-permute-start.44
  314.0 15.7 %collective-permute-done.45 = bf16[1024,512]{1,0:T(8,128)(2,1)S(1)} collective-permute-done((bf16[1024,512]{1,0:T(8,128)(2,1)S(1)}, bf16[1024,512]{1,0:T(8,128)(2,1)S(1)}, u32[]{:S(2)}, u32[]{:S(2)}) %collective-permute-start.45) | collective-permute-done | bytes 1048608 | tf_op jit(solution)/shard_map/ppermute | solution.py:28
  339.0 4.2 %collective-permute-done.46 = bf16[512,512]{1,0:T(8,128)(2,1)S(1)} collective-permute-done((bf16[512,512]{1,0:T(8,128)(2,1)S(1)}, bf16[512,512]{1,0:T(8,128)(2,1)S(1)}, u32[]{:S(2)}, u32[]{:S(2)}) %collective-permute-start.46) | collective-permute-done | bytes 524320 | tf_op jit(solution)/shard_map/ppermute | solution.py:24
  343.1 4.9 %collective-permute-done.48 = bf16[512,512]{1,0:T(8,128)(2,1)S(1)} collective-permute-done((bf16[512,512]{1,0:T(8,128)(2,1)S(1)}, bf16[512,512]{1,0:T(8,128)(2,1)S(1)}, u32[]{:S(2)}, u32[]{:S(2)}) %collective-permute-start.48) | collective-permute-done | bytes 524320 | tf_op jit(solution)/shard_map/ppermute | solution.py:28
  (212 shorter events, 118.7 us)
Async XLA Ops:
  7.2 189.1 %all-gather.3.cloned.1.call-start = ((), (), s32[]{:S(2)}) async-start(), calls=%async_computation | async-start | bytes 14155776 | tf_op jit(solution)/shard_map/all_gather | solution.py:541
  9.2 13.9 %collective-permute-start = (bf16[128,1536]{1,0:T(8,128)(2,1)}, bf16[128,1536]{1,0:T(8,128)(2,1)S(1)}, u32[]{:S(2)}, u32[]{:S(2)}) collective-permute-start(bf16[128,1536]{1,0:T(8,128)(2,1)} %prepare.1), channel_id=1, source_target_pairs={{0,3},{1,0},{2,1},{3,2},{4,7},{5,4},{6,5},{7,6},{8,11},{9,8},{10,9... | collective-permute-start | bytes 1179656 | tf_op jit(solution)/shard_map/ppermute | solution.py:28
  13.3 15.6 %collective-permute-start.1 = (bf16[128,1536]{1,0:T(8,128)(2,1)}, bf16[128,1536]{1,0:T(8,128)(2,1)S(1)}, u32[]{:S(2)}, u32[]{:S(2)}) collective-permute-start(bf16[128,1536]{1,0:T(8,128)(2,1)} %prepare.1), channel_id=1, source_target_pairs={{0,4},{1,5},{2,6},{3,7},{4,0},{5,1},{6,2},{7,3},{8,12},{9,13},{10,... | collective-permute-start | bytes 1179656 | tf_op jit(solution)/shard_map/ppermute | solution.py:24
  14.1 13.5 %collective-permute-start.2 = (bf16[128,1536]{1,0:T(8,128)(2,1)}, bf16[128,1536]{1,0:T(8,128)(2,1)S(1)}, u32[]{:S(2)}, u32[]{:S(2)}) collective-permute-start(bf16[128,1536]{1,0:T(8,128)(2,1)} %prepare.1), channel_id=1, source_target_pairs={{0,1},{1,2},{2,3},{3,0},{4,5},{5,6},{6,7},{7,4},{8,9},{9,10},{10,1... | collective-permute-start | bytes 1179656 | tf_op jit(solution)/shard_map/ppermute | solution.py:28
  15.4 34.2 %collective-permute-start.15 = (bf16[208,512]{1,0:T(8,128)(2,1)S(1)}, bf16[208,512]{1,0:T(8,128)(2,1)S(1)}, u32[]{:S(2)}, u32[]{:S(2)}) collective-permute-start(bf16[208,512]{1,0:T(8,128)(2,1)S(1)} %pad_maximum_fusion.14), channel_id=1, source_target_pairs={{0,3},{1,0},{2,1},{3,2},{4,7},{5,4},{6,5},{7,6},{8,11},{9,8},{10,9... | collective-permute-start | bytes 638984 | tf_op jit(solution)/shard_map/ppermute | solution.py:28
  18.6 31.0 %collective-permute-start.16 = (bf16[208,512]{1,0:T(8,128)(2,1)S(1)}, bf16[208,512]{1,0:T(8,128)(2,1)}, u32[]{:S(2)}, u32[]{:S(2)}) collective-permute-start(bf16[208,512]{1,0:T(8,128)(2,1)S(1)} %pad_maximum_fusion.14), channel_id=1, source_target_pairs={{0,1},{1,2},{2,3},{3,0},{4,5},{5,6},{6,7},{7,4},{8,9},{9,10},{10,1... | collective-permute-start | bytes 638984 | tf_op jit(solution)/shard_map/ppermute | solution.py:28
  23.1 28.4 %collective-permute-start.14 = (bf16[208,512]{1,0:T(8,128)(2,1)S(1)}, bf16[208,512]{1,0:T(8,128)(2,1)S(1)}, u32[]{:S(2)}, u32[]{:S(2)}) collective-permute-start(bf16[208,512]{1,0:T(8,128)(2,1)S(1)} %pad_maximum_fusion.14), channel_id=1, source_target_pairs={{0,4},{1,5},{2,6},{3,7},{4,0},{5,1},{6,2},{7,3},{8,12},{9,13},{10,... | collective-permute-start | bytes 638984 | tf_op jit(solution)/shard_map/ppermute | solution.py:24
  27.6 18.2 %collective-permute-start.4 = (bf16[256,1536]{1,0:T(8,128)(2,1)S(1)}, bf16[256,1536]{1,0:T(8,128)(2,1)S(1)}, u32[]{:S(2)}, u32[]{:S(2)}) collective-permute-start(bf16[256,1536]{1,0:T(8,128)(2,1)S(1)} %pad_maximum_fusion.7), channel_id=1, source_target_pairs={{0,4},{1,5},{2,6},{3,7},{4,0},{5,1},{6,2},{7,3},{8,12},{9,13},{10,... | collective-permute-start | bytes 2359304 | tf_op jit(solution)/shard_map/ppermute | solution.py:24
  29.0 17.4 %collective-permute-start.3 = (bf16[256,1536]{1,0:T(8,128)(2,1)S(1)}, bf16[256,1536]{1,0:T(8,128)(2,1)S(1)}, u32[]{:S(2)}, u32[]{:S(2)}) collective-permute-start(bf16[256,1536]{1,0:T(8,128)(2,1)S(1)} %pad_maximum_fusion.6), channel_id=1, source_target_pairs={{0,2},{1,3},{2,0},{3,1},{4,6},{5,7},{6,4},{7,5},{8,10},{9,11},{10,... | collective-permute-start | bytes 2359304 | tf_op jit(solution)/shard_map/ppermute | solution.py:28
  50.6 19.2 %collective-permute-start.18 = (bf16[416,512]{1,0:T(8,128)(2,1)S(1)}, bf16[416,512]{1,0:T(8,128)(2,1)S(1)}, u32[]{:S(2)}, u32[]{:S(2)}) collective-permute-start(bf16[416,512]{1,0:T(8,128)(2,1)S(1)} %maximum_add_fusion.1), channel_id=1, source_target_pairs={{0,4},{1,5},{2,6},{3,7},{4,0},{5,1},{6,2},{7,3},{8,12},{9,13},{10,... | collective-permute-start | bytes 1277960 | tf_op jit(solution)/shard_map/ppermute | solution.py:24
  51.6 18.2 %collective-permute-start.17 = (bf16[416,512]{1,0:T(8,128)(2,1)S(1)}, bf16[416,512]{1,0:T(8,128)(2,1)S(1)}, u32[]{:S(2)}, u32[]{:S(2)}) collective-permute-start(bf16[416,512]{1,0:T(8,128)(2,1)S(1)} %maximum_add_fusion), channel_id=1, source_target_pairs={{0,2},{1,3},{2,0},{3,1},{4,6},{5,7},{6,4},{7,5},{8,10},{9,11},{10,... | collective-permute-start | bytes 1277960 | tf_op jit(solution)/shard_map/ppermute | solution.py:28
  53.5 12.7 %collective-permute-start.5 = (bf16[512,384]{1,0:T(8,128)(2,1)S(1)}, bf16[512,384]{1,0:T(8,128)(2,1)S(1)}, u32[]{:S(2)}, u32[]{:S(2)}) collective-permute-start(bf16[512,384]{1,0:T(8,128)(2,1)S(1)} %get-tuple-element.14), channel_id=1, source_target_pairs={{0,8},{8,16},{16,24},{24,32},{32,40},{40,48},{48,56},{56,64},{64,7... | collective-permute-start | bytes 1179656 | tf_op jit(solution)/shard_map/ppermute | solution.py:532
  71.8 16.6 %collective-permute-start.6 = (bf16[256,1536]{1,0:T(8,128)(2,1)S(1)}, bf16[256,1536]{1,0:T(8,128)(2,1)S(1)}, u32[]{:S(2)}, u32[]{:S(2)}) collective-permute-start(bf16[256,1536]{1,0:T(8,128)(2,1)S(1)} %get-tuple-element.49), channel_id=1, source_target_pairs={{0,2},{1,3},{2,0},{3,1},{4,6},{5,7},{6,4},{7,5},{8,10},{9,11},{10,... | collective-permute-start | bytes 2359304 | tf_op jit(solution)/shard_map/ppermute | solution.py:28
  74.4 14.8 %collective-permute-start.8 = (bf16[256,1536]{1,0:T(8,128)(2,1)S(1)}, bf16[256,1536]{1,0:T(8,128)(2,1)S(1)}, u32[]{:S(2)}, u32[]{:S(2)}) collective-permute-start(bf16[256,1536]{1,0:T(8,128)(2,1)S(1)} %get-tuple-element.50), channel_id=1, source_target_pairs={{0,4},{1,5},{2,6},{3,7},{4,0},{5,1},{6,2},{7,3},{8,12},{9,13},{10,... | collective-permute-start | bytes 2359304 | tf_op jit(solution)/shard_map/ppermute | solution.py:24
  107.5 12.1 %collective-permute-start.12 = (bf16[128,1536]{1,0:T(8,128)(2,1)S(1)}, bf16[128,1536]{1,0:T(8,128)(2,1)S(1)}, u32[]{:S(2)}, u32[]{:S(2)}) collective-permute-start(bf16[128,1536]{1,0:T(8,128)(2,1)S(1)} %fusion.7), channel_id=1, source_target_pairs={{0,3},{1,0},{2,1},{3,2},{4,7},{5,4},{6,5},{7,6},{8,11},{9,8},{10,9... | collective-permute-start | bytes 1179656 | tf_op jit(solution)/shard_map/ppermute | solution.py:28
  107.6 17.5 %collective-permute-start.13 = (bf16[128,1536]{1,0:T(8,128)(2,1)S(1)}, bf16[128,1536]{1,0:T(8,128)(2,1)S(1)}, u32[]{:S(2)}, u32[]{:S(2)}) collective-permute-start(bf16[128,1536]{1,0:T(8,128)(2,1)S(1)} %fusion.7), channel_id=1, source_target_pairs={{0,1},{1,2},{2,3},{3,0},{4,5},{5,6},{6,7},{7,4},{8,9},{9,10},{10,1... | collective-permute-start | bytes 1179656 | tf_op jit(solution)/shard_map/ppermute | solution.py:28
  109.9 15.3 %collective-permute-start.11 = (bf16[128,1536]{1,0:T(8,128)(2,1)S(1)}, bf16[128,1536]{1,0:T(8,128)(2,1)S(1)}, u32[]{:S(2)}, u32[]{:S(2)}) collective-permute-start(bf16[128,1536]{1,0:T(8,128)(2,1)S(1)} %fusion.7), channel_id=1, source_target_pairs={{0,4},{1,5},{2,6},{3,7},{4,0},{5,1},{6,2},{7,3},{8,12},{9,13},{10,... | collective-permute-start | bytes 1179656 | tf_op jit(solution)/shard_map/ppermute | solution.py:24
  125.2 15.3 %collective-permute-start.20 = (bf16[256,1536]{1,0:T(8,128)(2,1)S(1)}, bf16[256,1536]{1,0:T(8,128)(2,1)S(1)}, u32[]{:S(2)}, u32[]{:S(2)}) collective-permute-start(bf16[256,1536]{1,0:T(8,128)(2,1)S(1)} %pad_maximum_fusion.9), channel_id=1, source_target_pairs={{0,4},{1,5},{2,6},{3,7},{4,0},{5,1},{6,2},{7,3},{8,12},{9,13},{10,... | collective-permute-start | bytes 2359304 | tf_op jit(solution)/shard_map/ppermute | solution.py:24
  125.3 18.0 %collective-permute-start.19 = (bf16[256,1536]{1,0:T(8,128)(2,1)S(1)}, bf16[256,1536]{1,0:T(8,128)(2,1)S(1)}, u32[]{:S(2)}, u32[]{:S(2)}) collective-permute-start(bf16[256,1536]{1,0:T(8,128)(2,1)S(1)} %pad_maximum_fusion.8), channel_id=1, source_target_pairs={{0,2},{1,3},{2,0},{3,1},{4,6},{5,7},{6,4},{7,5},{8,10},{9,11},{10,... | collective-permute-start | bytes 2359304 | tf_op jit(solution)/shard_map/ppermute | solution.py:28
  148.3 11.6 %collective-permute-start.21 = (bf16[128,1536]{1,0:T(8,128)(2,1)S(1)}, bf16[128,1536]{1,0:T(8,128)(2,1)S(1)}, u32[]{:S(2)}, u32[]{:S(2)}) collective-permute-start(bf16[128,1536]{1,0:T(8,128)(2,1)S(1)} %get-tuple-element.46), channel_id=1, source_target_pairs={{0,2},{1,3},{2,0},{3,1},{4,6},{5,7},{6,4},{7,5},{8,10},{9,11},{10,... | collective-permute-start | bytes 1179656 | tf_op jit(solution)/shard_map/ppermute | solution.py:28
  217.7 13.7 %collective-permute-start.33 = (bf16[528,384]{1,0:T(8,128)(2,1)S(1)}, bf16[528,384]{1,0:T(8,128)(2,1)S(1)}, u32[]{:S(2)}, u32[]{:S(2)}) collective-permute-start(bf16[528,384]{1,0:T(8,128)(2,1)S(1)} %get-tuple-element.39), channel_id=1, source_target_pairs={{0,16},{8,24},{16,32},{24,40},{32,48},{40,56},{48,0},{56,8},{64,80... | collective-permute-start | bytes 1216520 | tf_op jit(solution)/shard_map/ppermute | solution.py:463
  232.2 29.2 %collective-permute-start.34 = (bf16[4,528,256]{2,1,0:T(8,128)(2,1)S(1)}, bf16[4,528,256]{2,1,0:T(8,128)(2,1)}, u32[]{:S(2)}, u32[]{:S(2)}) collective-permute-start(bf16[4,528,256]{2,1,0:T(8,128)(2,1)S(1)} %pad_maximum_fusion.2.kv), channel_id=1, source_target_pairs={{0,64},{8,72},{16,80},{24,88},{32,96},{40,104},{48,112},{56,120},{... | collective-permute-start | bytes 3244040 | tf_op jit(solution)/shard_map/ppermute | solution.py:585
  263.4 41.6 %collective-permute-start.40 = (bf16[256,1536]{1,0:T(8,128)(2,1)}, bf16[256,1536]{1,0:T(8,128)(2,1)}, u32[]{:S(2)}, u32[]{:S(2)}) collective-permute-start(bf16[256,1536]{1,0:T(8,128)(2,1)} %get-tuple-element.43), channel_id=1, source_target_pairs={{0,2},{1,3},{2,0},{3,1},{4,6},{5,7},{6,4},{7,5},{8,10},{9,11},{10,... | collective-permute-start | bytes 2359304 | tf_op jit(solution)/shard_map/ppermute | solution.py:28
  263.4 41.6 %collective-permute-start.42 = (bf16[256,1536]{1,0:T(8,128)(2,1)}, bf16[256,1536]{1,0:T(8,128)(2,1)S(1)}, u32[]{:S(2)}, u32[]{:S(2)}) collective-permute-start(bf16[256,1536]{1,0:T(8,128)(2,1)} %get-tuple-element.44), channel_id=1, source_target_pairs={{0,4},{1,5},{2,6},{3,7},{4,0},{5,1},{6,2},{7,3},{8,12},{9,13},{10,... | collective-permute-start | bytes 2359304 | tf_op jit(solution)/shard_map/ppermute | solution.py:24
  298.3 31.4 %collective-permute-start.47 = (bf16[1024,512]{1,0:T(8,128)(2,1)S(1)}, bf16[1024,512]{1,0:T(8,128)(2,1)S(1)}, u32[]{:S(2)}, u32[]{:S(2)}) collective-permute-start(bf16[1024,512]{1,0:T(8,128)(2,1)S(1)} %output_columns.3), channel_id=1, source_target_pairs={{0,4},{1,5},{2,6},{3,7},{4,0},{5,1},{6,2},{7,3},{8,12},{9,13},{10,... | collective-permute-start | bytes 3145736 | tf_op jit(solution)/shard_map/ppermute | solution.py:24
  302.0 27.7 %collective-permute-start.45 = (bf16[1024,512]{1,0:T(8,128)(2,1)S(1)}, bf16[1024,512]{1,0:T(8,128)(2,1)S(1)}, u32[]{:S(2)}, u32[]{:S(2)}) collective-permute-start(bf16[1024,512]{1,0:T(8,128)(2,1)S(1)} %output_columns.5), channel_id=1, source_target_pairs={{0,2},{1,3},{2,0},{3,1},{4,6},{5,7},{6,4},{7,5},{8,10},{9,11},{10,... | collective-permute-start | bytes 3145736 | tf_op jit(solution)/shard_map/ppermute | solution.py:28
  306.3 26.6 %collective-permute-start.41 = (bf16[128,1536]{1,0:T(8,128)(2,1)S(1)}, bf16[128,1536]{1,0:T(8,128)(2,1)S(1)}, u32[]{:S(2)}, u32[]{:S(2)}) collective-permute-start(bf16[128,1536]{1,0:T(8,128)(2,1)S(1)} %get-tuple-element.42), channel_id=1, source_target_pairs={{0,4},{1,5},{2,6},{3,7},{4,0},{5,1},{6,2},{7,3},{8,12},{9,13},{10,... | collective-permute-start | bytes 1179656 | tf_op jit(solution)/shard_map/ppermute | solution.py:24
  308.1 28.8 %collective-permute-start.43 = (bf16[128,1536]{1,0:T(8,128)(2,1)S(1)}, bf16[128,1536]{1,0:T(8,128)(2,1)S(1)}, u32[]{:S(2)}, u32[]{:S(2)}) collective-permute-start(bf16[128,1536]{1,0:T(8,128)(2,1)S(1)} %get-tuple-element.30), channel_id=1, source_target_pairs={{0,1},{1,2},{2,3},{3,0},{4,5},{5,6},{6,7},{7,4},{8,9},{9,10},{10,1... | collective-permute-start | bytes 1179656 | tf_op jit(solution)/shard_map/ppermute | solution.py:28
  308.1 28.8 %collective-permute-start.44 = (bf16[128,1536]{1,0:T(8,128)(2,1)S(1)}, bf16[128,1536]{1,0:T(8,128)(2,1)S(1)}, u32[]{:S(2)}, u32[]{:S(2)}) collective-permute-start(bf16[128,1536]{1,0:T(8,128)(2,1)S(1)} %get-tuple-element.31), channel_id=1, source_target_pairs={{0,3},{1,0},{2,1},{3,2},{4,7},{5,4},{6,5},{7,6},{8,11},{9,8},{10,9... | collective-permute-start | bytes 1179656 | tf_op jit(solution)/shard_map/ppermute | solution.py:28
  330.2 13.0 %collective-permute-start.46 = (bf16[512,512]{1,0:T(8,128)(2,1)S(1)}, bf16[512,512]{1,0:T(8,128)(2,1)S(1)}, u32[]{:S(2)}, u32[]{:S(2)}) collective-permute-start(bf16[512,512]{1,0:T(8,128)(2,1)S(1)} %get-tuple-element.34), channel_id=1, source_target_pairs={{0,4},{1,5},{2,6},{3,7},{4,0},{5,1},{6,2},{7,3},{8,12},{9,13},{10,... | collective-permute-start | bytes 1572872 | tf_op jit(solution)/shard_map/ppermute | solution.py:24
  330.8 17.2 %collective-permute-start.48 = (bf16[512,512]{1,0:T(8,128)(2,1)S(1)}, bf16[512,512]{1,0:T(8,128)(2,1)S(1)}, u32[]{:S(2)}, u32[]{:S(2)}) collective-permute-start(bf16[512,512]{1,0:T(8,128)(2,1)S(1)} %get-tuple-element.26), channel_id=1, source_target_pairs={{0,1},{1,2},{2,3},{3,0},{4,5},{5,6},{6,7},{7,4},{8,9},{9,10},{10,1... | collective-permute-start | bytes 1572872 | tf_op jit(solution)/shard_map/ppermute | solution.py:28
  332.8 15.2 %collective-permute-start.49 = (bf16[512,512]{1,0:T(8,128)(2,1)S(1)}, bf16[512,512]{1,0:T(8,128)(2,1)S(1)}, u32[]{:S(2)}, u32[]{:S(2)}) collective-permute-start(bf16[512,512]{1,0:T(8,128)(2,1)S(1)} %get-tuple-element.27), channel_id=1, source_target_pairs={{0,3},{1,0},{2,1},{3,2},{4,7},{5,4},{6,5},{7,6},{8,11},{9,8},{10,9... | collective-permute-start | bytes 1572872 | tf_op jit(solution)/shard_map/ppermute | solution.py:28
  (49 other events, 371.7 us)
Sparse Core Ops, SparseCore 0:
  71.2 65.1 all-gather.2

commit v3 on v0

--- a/solution.py
+++ b/solution.py
@@ -585,7 +585,8 @@
     first_kv = lax.ppermute(own_kv, "seq", [(i, i + 8) for i in range(8)])
     info_two = jnp.stack([half, core, y]).astype(jnp.int32)
     running = causal_attend(True, info_two, queries, (own_kv, flip_seq(own_kv, 1)))
-    first_kv = first_kv + running[1][0, 2, 0].astype(BF16)
+    unread = jnp.broadcast_to(running[1][0:1, 2:3, :128], (1, EXT, 128)).astype(BF16)
+    first_kv = lax.dynamic_update_slice(first_kv, unread, (0, capacity, 128))
     mixed = causal_attend(False, info_two, queries, (first_kv, flip_seq(first_kv, 1)), running)
     back = [mixed[0], turn_y(mixed[3], 3), turn_y(mixed[2], 2), turn_y(mixed[1], 1)]
     out_opposite = turn_z(output_columns(block_of[4:6], y, back, heads_out_two), 2)

time: 354 us -> 354 us (level)
  no operation moved by 1% of the time
where the time goes in v3:
time: 354 us; the launch traced here: 347 us
  waiting for transfers between devices  163 us (46%)
  Pallas kernels  73.7 us (21%)
  starting transfers between devices  56.8 us (16%)
  between operations  19.8 us (6%)
  local copies, waits for them, and re-layouts  16.3 us (5%)
  other arithmetic  13.7 us (4%)
  matrix products  3.73 us (1%)
    ppermute x24, waiting for transfers between devices, turn_z(): lax.ppermute(value, 'blk', [(i, i & 4 | i + steps & 3) for i in range(8)])  95 us
    ppermute x16, waiting for transfers between devices, flip_x(): return lax.ppermute(value, 'blk', [(i, i ^ 4) for i in range(8)])  34.5 us
    ppermute x24, starting transfers between devices, turn_z(): lax.ppermute(value, 'blk', [(i, i & 4 | i + steps & 3) for i in range(8)])  33.6 us
    pallas_call x2, Pallas kernels, causal_attend(): pl.pallas_call(kernel, out_shape=out_shape, grid_spec=pltpu.PrefetchScala...  30.1 us
    pallas_call x1, Pallas kernels, project_two(): pl.pallas_call(project_kernel, out_shape=(jax.ShapeDtypeStruct((4, 512 +...  18.2 us
    ppermute x16, starting transfers between devices, flip_x(): return lax.ppermute(value, 'blk', [(i, i ^ 4) for i in range(8)])  15.3 us
    ppermute x6, waiting for transfers between devices, turn_y(): lax.ppermute(value, 'seq', [(i, i & 9 | i + 2 * steps & 6) for i in range...  13.8 us
    ppermute x1, waiting for transfers between devices, per_device(): first_kv = lax.ppermute(own_kv, 'seq', [(i, i + 8) for i in range(8)])  12.5 us
  transfers between devices with their start and end apart: 51, of which 32 were waited for; matrix products, arithmetic and copies ran while one was open for 6% of the time, Pallas kernels for 15%

profile of v3, /device:TPU:6, one launch (start us, length us, event | category | flops | bytes accessed | tf_op | source)
XLA Modules:
  0.0 347.4 jit_solution(14505975776171770024)
XLA Ops:
  9.2 4.0 %collective-permute-start = (bf16[128,1536]{1,0:T(8,128)(2,1)}, bf16[128,1536]{1,0:T(8,128)(2,1)S(1)}, u32[]{:S(2)}, u32[]{:S(2)}) collective-permute-start(bf16[128,1536]{1,0:T(8,128)(2,1)} %prepare.1), channel_id=1, source_target_pairs={{0,3},{1,0},{2,1},{3,2},{4,7},{5,4},{6,5},{7,6},{8,11},{9,8},{10,9... | collective-permute-start | bytes 1179656 | tf_op jit(solution)/shard_map/ppermute | solution.py:28
  15.4 3.2 collective-permute-start.15
  18.8 4.3 %collective-permute-done = bf16[128,1536]{1,0:T(8,128)(2,1)S(1)} collective-permute-done((bf16[128,1536]{1,0:T(8,128)(2,1)}, bf16[128,1536]{1,0:T(8,128)(2,1)S(1)}, u32[]{:S(2)}, u32[]{:S(2)}) %collective-permute-start) | collective-permute-done | bytes 393248 | tf_op jit(solution)/shard_map/ppermute | solution.py:28
  23.9 3.6 %collective-permute-done.2 = bf16[128,1536]{1,0:T(8,128)(2,1)S(1)} collective-permute-done((bf16[128,1536]{1,0:T(8,128)(2,1)}, bf16[128,1536]{1,0:T(8,128)(2,1)S(1)}, u32[]{:S(2)}, u32[]{:S(2)}) %collective-permute-start.2) | collective-permute-done | bytes 393248 | tf_op jit(solution)/shard_map/ppermute | solution.py:28
  35.5 10.3 %collective-permute-done.4.diagonal = bf16[256,1536]{1,0:T(8,128)(2,1)S(1)} collective-permute-done((bf16[256,1536]{1,0:T(8,128)(2,1)S(1)}, bf16[256,1536]{1,0:T(8,128)(2,1)S(1)}, u32[]{:S(2)}, u32[]{:S(2)}) %collective-permute-start.4) | collective-permute-done | bytes 786464 | tf_op jit(solution)/shard_map/ppermute | solution.py:24
  55.6 3.5 %window_late.1.before = bf16[1024,192]{1,0:T(8,128)(2,1)S(1)} custom-call(s32[9]{0:T(128)S(1)} %add_add_fusion.info, bf16[1024,576]{1,0:T(8,128)(2,1)S(1)} %get-tuple-element.13.qkv), custom_call_target="tpu_custom_call" | custom-call | flops 251658240 | bytes 2097152 | tf_op jit(solution)/shard_map/window_late/pallas_call | solution.py:143
  59.2 7.0 %collective-permute-done.5.halo = bf16[512,384]{1,0:T(8,128)(2,1)S(1)} collective-permute-done((bf16[512,384]{1,0:T(8,128)(2,1)S(1)}, bf16[512,384]{1,0:T(8,128)(2,1)S(1)}, u32[]{:S(2)}, u32[]{:S(2)}) %collective-permute-start.5) | collective-permute-done | bytes 393248 | tf_op jit(solution)/shard_map/ppermute | solution.py:532
  66.2 3.6 %window_early.1._ = bf16[1024,192]{1,0:T(8,128)(2,1)S(1)} custom-call(s32[9]{0:T(128)S(1)} %add_add_fusion.info, bf16[1024,576]{1,0:T(8,128)(2,1)S(1)} %get-tuple-element.13.qkv, bf16[512,384]{1,0:T(8,128)(2,1)S(1)} %collective-permute-done.5.halo, bf16[1024,192]{1,0:T(8,128)(2,1)S(1)} %window_late.1.before), custom_call_target="tpu_custom_call" | custom-call | flops 251658240 | bytes 2097152 | tf_op jit(solution)/shard_map/window_early/pallas_call | solution.py:143
  75.4 13.0 %collective-permute-done.6 = bf16[256,1536]{1,0:T(8,128)(2,1)S(1)} collective-permute-done((bf16[256,1536]{1,0:T(8,128)(2,1)S(1)}, bf16[256,1536]{1,0:T(8,128)(2,1)S(1)}, u32[]{:S(2)}, u32[]{:S(2)}) %collective-permute-start.6) | collective-permute-done | bytes 786464 | tf_op jit(solution)/shard_map/ppermute | solution.py:28
  89.5 3.8 %collective-permute-start.10 = (bf16[128,1536]{1,0:T(8,128)(2,1)S(1)}, bf16[128,1536]{1,0:T(8,128)(2,1)}, u32[]{:S(2)}, u32[]{:S(2)}) collective-permute-start(bf16[128,1536]{1,0:T(8,128)(2,1)S(1)} %get-tuple-element.33), channel_id=1, source_target_pairs={{0,3},{1,0},{2,1},{3,2},{4,7},{5,4},{6,5},{7,6},{8,11},{9,8},{10,9... | collective-permute-start | bytes 1179656 | tf_op jit(solution)/shard_map/ppermute | solution.py:28
  94.8 5.1 %collective-permute-done.10 = bf16[128,1536]{1,0:T(8,128)(2,1)} collective-permute-done((bf16[128,1536]{1,0:T(8,128)(2,1)S(1)}, bf16[128,1536]{1,0:T(8,128)(2,1)}, u32[]{:S(2)}, u32[]{:S(2)}) %collective-permute-start.10) | collective-permute-done | bytes 393248 | tf_op jit(solution)/shard_map/ppermute | solution.py:28
  101.4 3.9 %collective-permute-done.9 = bf16[128,1536]{1,0:T(8,128)(2,1)} collective-permute-done((bf16[128,1536]{1,0:T(8,128)(2,1)S(1)}, bf16[128,1536]{1,0:T(8,128)(2,1)}, u32[]{:S(2)}, u32[]{:S(2)}) %collective-permute-start.9) | collective-permute-done | bytes 393248 | tf_op jit(solution)/shard_map/ppermute | solution.py:28
  111.6 8.1 %collective-permute-done.12 = bf16[128,1536]{1,0:T(8,128)(2,1)S(1)} collective-permute-done((bf16[128,1536]{1,0:T(8,128)(2,1)S(1)}, bf16[128,1536]{1,0:T(8,128)(2,1)S(1)}, u32[]{:S(2)}, u32[]{:S(2)}) %collective-permute-start.12) | collective-permute-done | bytes 393248 | tf_op jit(solution)/shard_map/ppermute | solution.py:28
  119.7 5.5 %collective-permute-done.13 = bf16[128,1536]{1,0:T(8,128)(2,1)S(1)} collective-permute-done((bf16[128,1536]{1,0:T(8,128)(2,1)S(1)}, bf16[128,1536]{1,0:T(8,128)(2,1)S(1)}, u32[]{:S(2)}, u32[]{:S(2)}) %collective-permute-start.13) | collective-permute-done | bytes 393248 | tf_op jit(solution)/shard_map/ppermute | solution.py:28
  128.2 3.0 mlp.2
  131.2 9.3 %collective-permute-done.20.refs_1_ = bf16[256,1536]{1,0:T(8,128)(2,1)S(1)} collective-permute-done((bf16[256,1536]{1,0:T(8,128)(2,1)S(1)}, bf16[256,1536]{1,0:T(8,128)(2,1)S(1)}, u32[]{:S(2)}, u32[]{:S(2)}) %collective-permute-start.20) | collective-permute-done | bytes 786464 | tf_op jit(solution)/shard_map/ppermute | solution.py:24
  150.5 9.4 %collective-permute-done.21 = bf16[128,1536]{1,0:T(8,128)(2,1)S(1)} collective-permute-done((bf16[128,1536]{1,0:T(8,128)(2,1)S(1)}, bf16[128,1536]{1,0:T(8,128)(2,1)S(1)}, u32[]{:S(2)}, u32[]{:S(2)}) %collective-permute-start.21) | collective-permute-done | bytes 393248 | tf_op jit(solution)/shard_map/ppermute | solution.py:28
  161.9 3.2 collective-permute-start.25
  168.8 3.3 collective-permute-done.25
  172.3 3.7 %collective-permute-start.27 = (bf16[64,1536]{1,0:T(8,128)(2,1)S(1)}, bf16[64,1536]{1,0:T(8,128)(2,1)S(1)}, u32[]{:S(2)}, u32[]{:S(2)}) collective-permute-start(bf16[64,1536]{1,0:T(8,128)(2,1)S(1)} %add_convert_fusion.10), channel_id=1, source_target_pairs={{0,3},{1,0},{2,1},{3,2},{4,7},{5,4},{6,5},{7,6},{8,11},{9,8},{10,9... | collective-permute-start | bytes 589832 | tf_op jit(solution)/shard_map/ppermute | solution.py:28
  176.3 2.9 collective-permute-done.27
  179.2 3.7 %collective-permute-done.28 = bf16[64,1536]{1,0:T(8,128)(2,1)S(1)} collective-permute-done((bf16[64,1536]{1,0:T(8,128)(2,1)S(1)}, bf16[64,1536]{1,0:T(8,128)(2,1)S(1)}, u32[]{:S(2)}, u32[]{:S(2)}) %collective-permute-start.28) | collective-permute-done | bytes 196640 | tf_op jit(solution)/shard_map/ppermute | solution.py:28
  187.9 4.5 %collective-permute-done.30.diagonal = bf16[128,1536]{1,0:T(8,128)(2,1)S(1)} collective-permute-done((bf16[128,1536]{1,0:T(8,128)(2,1)}, bf16[128,1536]{1,0:T(8,128)(2,1)S(1)}, u32[]{:S(2)}, u32[]{:S(2)}) %collective-permute-start.30) | collective-permute-done | bytes 393248 | tf_op jit(solution)/shard_map/ppermute | solution.py:24
  198.3 18.2 %project_two.1 = (bf16[4,528,384]{2,1,0:T(8,128)(2,1)S(1)}, bf16[512,512]{1,0:T(8,128)(2,1)S(1)}) custom-call(s32[9]{0:T(128)S(1)} %concatenate.73.info, bf16[256,1536]{1,0:T(8,128)(2,1)S(1)} %pad_maximum_fusion.10.near, bf16[128,1536]{1,0:T(8,128)(2,1)S(1)} %copy-done.12, bf16[128,1536]{1,0:T(8,128)(2,1)S(1)} %copy-done.10, ...), custom_call_target="tpu_custom_call" | custom-call | flops 12884901888 | bytes 29360128 | tf_op jit(solution)/shard_map/project_two/pallas_call | solution.py:314
  219.8 5.6 %collective-permute-done.31 = bf16[528,384]{1,0:T(8,128)(2,1)S(1)} collective-permute-done((bf16[528,384]{1,0:T(8,128)(2,1)S(1)}, bf16[528,384]{1,0:T(8,128)(2,1)S(1)}, u32[]{:S(2)}, u32[]{:S(2)}) %collective-permute-start.31) | collective-permute-done | bytes 405536 | tf_op jit(solution)/shard_map/ppermute | solution.py:463
  227.3 4.2 %collective-permute-done.33 = bf16[528,384]{1,0:T(8,128)(2,1)S(1)} collective-permute-done((bf16[528,384]{1,0:T(8,128)(2,1)S(1)}, bf16[528,384]{1,0:T(8,128)(2,1)S(1)}, u32[]{:S(2)}, u32[]{:S(2)}) %collective-permute-start.33) | collective-permute-done | bytes 405536 | tf_op jit(solution)/shard_map/ppermute | solution.py:463
  236.7 12.3 %causal_own.1 = (f32[4,128,512]{2,1,0:T(8,128)S(1)}, f32[4,8,512]{2,1,0:T(8,128)S(1)}) custom-call(s32[3]{0:T(128)S(1)} %add_add_fusion.1.info, bf16[4,512,128]{2,1,0:T(8,128)(2,1)S(1)} %pad_maximum_fusion.11.queries, bf16[4,528,256]{2,1,0:T(8,128)(2,1)S(1)} %pad_maximum_fusion.2.kv, bf16[4,528,256]{2,1,0:T(8,128)(2,1)} %collective-permute-done.35.other), custom_call_target="tpu_custom_call" | custom-call | flops 2415919104 | bytes 4194304 | tf_op jit(solution)/shard_map/causal_own/pallas_call | solution.py:439
  249.0 12.5 %collective-permute-done.34 = bf16[4,528,256]{2,1,0:T(8,128)(2,1)} collective-permute-done((bf16[4,528,256]{2,1,0:T(8,128)(2,1)S(1)}, bf16[4,528,256]{2,1,0:T(8,128)(2,1)}, u32[]{:S(2)}, u32[]{:S(2)}) %collective-permute-start.34) | collective-permute-done | bytes 1081376 | tf_op jit(solution)/shard_map/ppermute | solution.py:585
  265.0 17.8 %causal_first_half.1 = bf16[4,512,128]{2,1,0:T(8,128)(2,1)S(1)} custom-call(s32[3]{0:T(128)S(1)} %add_add_fusion.1.info, bf16[4,512,128]{2,1,0:T(8,128)(2,1)S(1)} %pad_maximum_fusion.11.queries, bf16[4,528,256]{2,1,0:T(8,128)(2,1)} %broadcast_dynamic-update-slice_fusion.kv, bf16[4,528,256]{2,1,0:T(8,128)(2,1)S(1)} %collective-permute-done.36.other, ...), custom_call_target="tpu_custom_call" | custom-call | flops 4294967296 | bytes 4194304 | tf_op jit(solution)/shard_map/causal_first_half/pallas_call | solution.py:439
  299.6 23.0 %collective-permute-done.40 = bf16[128,1536]{1,0:T(8,128)(2,1)S(1)} collective-permute-done((bf16[128,1536]{1,0:T(8,128)(2,1)S(1)}, bf16[128,1536]{1,0:T(8,128)(2,1)S(1)}, u32[]{:S(2)}, u32[]{:S(2)}) %collective-permute-start.40) | collective-permute-done | bytes 393248 | tf_op jit(solution)/shard_map/ppermute | solution.py:28
  327.6 3.2 collective-permute-start.49
  330.8 6.6 %collective-permute-done.46 = bf16[512,512]{1,0:T(8,128)(2,1)S(1)} collective-permute-done((bf16[512,512]{1,0:T(8,128)(2,1)S(1)}, bf16[512,512]{1,0:T(8,128)(2,1)S(1)}, u32[]{:S(2)}, u32[]{:S(2)}) %collective-permute-start.46) | collective-permute-done | bytes 524320 | tf_op jit(solution)/shard_map/ppermute | solution.py:24
  (214 shorter events, 102.3 us)
Async XLA Ops:
  7.2 189.1 %all-gather.3.cloned.1.call-start = ((), (), s32[]{:S(2)}) async-start(), calls=%async_computation | async-start | bytes 14155776 | tf_op jit(solution)/shard_map/all_gather | solution.py:541
  9.2 13.9 %collective-permute-start = (bf16[128,1536]{1,0:T(8,128)(2,1)}, bf16[128,1536]{1,0:T(8,128)(2,1)S(1)}, u32[]{:S(2)}, u32[]{:S(2)}) collective-permute-start(bf16[128,1536]{1,0:T(8,128)(2,1)} %prepare.1), channel_id=1, source_target_pairs={{0,3},{1,0},{2,1},{3,2},{4,7},{5,4},{6,5},{7,6},{8,11},{9,8},{10,9... | collective-permute-start | bytes 1179656 | tf_op jit(solution)/shard_map/ppermute | solution.py:28
  13.3 15.6 %collective-permute-start.1 = (bf16[128,1536]{1,0:T(8,128)(2,1)}, bf16[128,1536]{1,0:T(8,128)(2,1)S(1)}, u32[]{:S(2)}, u32[]{:S(2)}) collective-permute-start(bf16[128,1536]{1,0:T(8,128)(2,1)} %prepare.1), channel_id=1, source_target_pairs={{0,4},{1,5},{2,6},{3,7},{4,0},{5,1},{6,2},{7,3},{8,12},{9,13},{10,... | collective-permute-start | bytes 1179656 | tf_op jit(solution)/shard_map/ppermute | solution.py:24
  14.1 13.5 %collective-permute-start.2 = (bf16[128,1536]{1,0:T(8,128)(2,1)}, bf16[128,1536]{1,0:T(8,128)(2,1)S(1)}, u32[]{:S(2)}, u32[]{:S(2)}) collective-permute-start(bf16[128,1536]{1,0:T(8,128)(2,1)} %prepare.1), channel_id=1, source_target_pairs={{0,1},{1,2},{2,3},{3,0},{4,5},{5,6},{6,7},{7,4},{8,9},{9,10},{10,1... | collective-permute-start | bytes 1179656 | tf_op jit(solution)/shard_map/ppermute | solution.py:28
  15.4 34.2 %collective-permute-start.15 = (bf16[208,512]{1,0:T(8,128)(2,1)S(1)}, bf16[208,512]{1,0:T(8,128)(2,1)S(1)}, u32[]{:S(2)}, u32[]{:S(2)}) collective-permute-start(bf16[208,512]{1,0:T(8,128)(2,1)S(1)} %pad_maximum_fusion.14), channel_id=1, source_target_pairs={{0,3},{1,0},{2,1},{3,2},{4,7},{5,4},{6,5},{7,6},{8,11},{9,8},{10,9... | collective-permute-start | bytes 638984 | tf_op jit(solution)/shard_map/ppermute | solution.py:28
  18.6 31.0 %collective-permute-start.16 = (bf16[208,512]{1,0:T(8,128)(2,1)S(1)}, bf16[208,512]{1,0:T(8,128)(2,1)}, u32[]{:S(2)}, u32[]{:S(2)}) collective-permute-start(bf16[208,512]{1,0:T(8,128)(2,1)S(1)} %pad_maximum_fusion.14), channel_id=1, source_target_pairs={{0,1},{1,2},{2,3},{3,0},{4,5},{5,6},{6,7},{7,4},{8,9},{9,10},{10,1... | collective-permute-start | bytes 638984 | tf_op jit(solution)/shard_map/ppermute | solution.py:28
  23.1 28.4 %collective-permute-start.14 = (bf16[208,512]{1,0:T(8,128)(2,1)S(1)}, bf16[208,512]{1,0:T(8,128)(2,1)S(1)}, u32[]{:S(2)}, u32[]{:S(2)}) collective-permute-start(bf16[208,512]{1,0:T(8,128)(2,1)S(1)} %pad_maximum_fusion.14), channel_id=1, source_target_pairs={{0,4},{1,5},{2,6},{3,7},{4,0},{5,1},{6,2},{7,3},{8,12},{9,13},{10,... | collective-permute-start | bytes 638984 | tf_op jit(solution)/shard_map/ppermute | solution.py:24
  27.6 18.2 %collective-permute-start.4 = (bf16[256,1536]{1,0:T(8,128)(2,1)S(1)}, bf16[256,1536]{1,0:T(8,128)(2,1)S(1)}, u32[]{:S(2)}, u32[]{:S(2)}) collective-permute-start(bf16[256,1536]{1,0:T(8,128)(2,1)S(1)} %pad_maximum_fusion.7), channel_id=1, source_target_pairs={{0,4},{1,5},{2,6},{3,7},{4,0},{5,1},{6,2},{7,3},{8,12},{9,13},{10,... | collective-permute-start | bytes 2359304 | tf_op jit(solution)/shard_map/ppermute | solution.py:24
  29.0 17.4 %collective-permute-start.3 = (bf16[256,1536]{1,0:T(8,128)(2,1)S(1)}, bf16[256,1536]{1,0:T(8,128)(2,1)S(1)}, u32[]{:S(2)}, u32[]{:S(2)}) collective-permute-start(bf16[256,1536]{1,0:T(8,128)(2,1)S(1)} %pad_maximum_fusion.6), channel_id=1, source_target_pairs={{0,2},{1,3},{2,0},{3,1},{4,6},{5,7},{6,4},{7,5},{8,10},{9,11},{10,... | collective-permute-start | bytes 2359304 | tf_op jit(solution)/shard_map/ppermute | solution.py:28
  50.6 19.2 %collective-permute-start.18 = (bf16[416,512]{1,0:T(8,128)(2,1)S(1)}, bf16[416,512]{1,0:T(8,128)(2,1)S(1)}, u32[]{:S(2)}, u32[]{:S(2)}) collective-permute-start(bf16[416,512]{1,0:T(8,128)(2,1)S(1)} %maximum_add_fusion.1), channel_id=1, source_target_pairs={{0,4},{1,5},{2,6},{3,7},{4,0},{5,1},{6,2},{7,3},{8,12},{9,13},{10,... | collective-permute-start | bytes 1277960 | tf_op jit(solution)/shard_map/ppermute | solution.py:24
  51.6 18.2 %collective-permute-start.17 = (bf16[416,512]{1,0:T(8,128)(2,1)S(1)}, bf16[416,512]{1,0:T(8,128)(2,1)S(1)}, u32[]{:S(2)}, u32[]{:S(2)}) collective-permute-start(bf16[416,512]{1,0:T(8,128)(2,1)S(1)} %maximum_add_fusion), channel_id=1, source_target_pairs={{0,2},{1,3},{2,0},{3,1},{4,6},{5,7},{6,4},{7,5},{8,10},{9,11},{10,... | collective-permute-start | bytes 1277960 | tf_op jit(solution)/shard_map/ppermute | solution.py:28
  53.5 12.7 %collective-permute-start.5 = (bf16[512,384]{1,0:T(8,128)(2,1)S(1)}, bf16[512,384]{1,0:T(8,128)(2,1)S(1)}, u32[]{:S(2)}, u32[]{:S(2)}) collective-permute-start(bf16[512,384]{1,0:T(8,128)(2,1)S(1)} %get-tuple-element.14), channel_id=1, source_target_pairs={{0,8},{8,16},{16,24},{24,32},{32,40},{40,48},{48,56},{56,64},{64,7... | collective-permute-start | bytes 1179656 | tf_op jit(solution)/shard_map/ppermute | solution.py:532
  71.8 16.6 %collective-permute-start.6 = (bf16[256,1536]{1,0:T(8,128)(2,1)S(1)}, bf16[256,1536]{1,0:T(8,128)(2,1)S(1)}, u32[]{:S(2)}, u32[]{:S(2)}) collective-permute-start(bf16[256,1536]{1,0:T(8,128)(2,1)S(1)} %get-tuple-element.49), channel_id=1, source_target_pairs={{0,2},{1,3},{2,0},{3,1},{4,6},{5,7},{6,4},{7,5},{8,10},{9,11},{10,... | collective-permute-start | bytes 2359304 | tf_op jit(solution)/shard_map/ppermute | solution.py:28
  74.4 14.8 %collective-permute-start.8 = (bf16[256,1536]{1,0:T(8,128)(2,1)S(1)}, bf16[256,1536]{1,0:T(8,128)(2,1)S(1)}, u32[]{:S(2)}, u32[]{:S(2)}) collective-permute-start(bf16[256,1536]{1,0:T(8,128)(2,1)S(1)} %get-tuple-element.50), channel_id=1, source_target_pairs={{0,4},{1,5},{2,6},{3,7},{4,0},{5,1},{6,2},{7,3},{8,12},{9,13},{10,... | collective-permute-start | bytes 2359304 | tf_op jit(solution)/shard_map/ppermute | solution.py:24
  94.0 11.3 %collective-permute-start.9 = (bf16[128,1536]{1,0:T(8,128)(2,1)S(1)}, bf16[128,1536]{1,0:T(8,128)(2,1)}, u32[]{:S(2)}, u32[]{:S(2)}) collective-permute-start(bf16[128,1536]{1,0:T(8,128)(2,1)S(1)} %get-tuple-element.32), channel_id=1, source_target_pairs={{0,1},{1,2},{2,3},{3,0},{4,5},{5,6},{6,7},{7,4},{8,9},{9,10},{10,1... | collective-permute-start | bytes 1179656 | tf_op jit(solution)/shard_map/ppermute | solution.py:28
  107.5 12.1 %collective-permute-start.12 = (bf16[128,1536]{1,0:T(8,128)(2,1)S(1)}, bf16[128,1536]{1,0:T(8,128)(2,1)S(1)}, u32[]{:S(2)}, u32[]{:S(2)}) collective-permute-start(bf16[128,1536]{1,0:T(8,128)(2,1)S(1)} %fusion.7), channel_id=1, source_target_pairs={{0,3},{1,0},{2,1},{3,2},{4,7},{5,4},{6,5},{7,6},{8,11},{9,8},{10,9... | collective-permute-start | bytes 1179656 | tf_op jit(solution)/shard_map/ppermute | solution.py:28
  107.6 17.5 %collective-permute-start.13 = (bf16[128,1536]{1,0:T(8,128)(2,1)S(1)}, bf16[128,1536]{1,0:T(8,128)(2,1)S(1)}, u32[]{:S(2)}, u32[]{:S(2)}) collective-permute-start(bf16[128,1536]{1,0:T(8,128)(2,1)S(1)} %fusion.7), channel_id=1, source_target_pairs={{0,1},{1,2},{2,3},{3,0},{4,5},{5,6},{6,7},{7,4},{8,9},{9,10},{10,1... | collective-permute-start | bytes 1179656 | tf_op jit(solution)/shard_map/ppermute | solution.py:28
  109.9 15.3 %collective-permute-start.11 = (bf16[128,1536]{1,0:T(8,128)(2,1)S(1)}, bf16[128,1536]{1,0:T(8,128)(2,1)S(1)}, u32[]{:S(2)}, u32[]{:S(2)}) collective-permute-start(bf16[128,1536]{1,0:T(8,128)(2,1)S(1)} %fusion.7), channel_id=1, source_target_pairs={{0,4},{1,5},{2,6},{3,7},{4,0},{5,1},{6,2},{7,3},{8,12},{9,13},{10,... | collective-permute-start | bytes 1179656 | tf_op jit(solution)/shard_map/ppermute | solution.py:24
  125.2 15.3 %collective-permute-start.20 = (bf16[256,1536]{1,0:T(8,128)(2,1)S(1)}, bf16[256,1536]{1,0:T(8,128)(2,1)S(1)}, u32[]{:S(2)}, u32[]{:S(2)}) collective-permute-start(bf16[256,1536]{1,0:T(8,128)(2,1)S(1)} %pad_maximum_fusion.9), channel_id=1, source_target_pairs={{0,4},{1,5},{2,6},{3,7},{4,0},{5,1},{6,2},{7,3},{8,12},{9,13},{10,... | collective-permute-start | bytes 2359304 | tf_op jit(solution)/shard_map/ppermute | solution.py:24
  125.3 18.0 %collective-permute-start.19 = (bf16[256,1536]{1,0:T(8,128)(2,1)S(1)}, bf16[256,1536]{1,0:T(8,128)(2,1)S(1)}, u32[]{:S(2)}, u32[]{:S(2)}) collective-permute-start(bf16[256,1536]{1,0:T(8,128)(2,1)S(1)} %pad_maximum_fusion.8), channel_id=1, source_target_pairs={{0,2},{1,3},{2,0},{3,1},{4,6},{5,7},{6,4},{7,5},{8,10},{9,11},{10,... | collective-permute-start | bytes 2359304 | tf_op jit(solution)/shard_map/ppermute | solution.py:28
  148.3 11.6 %collective-permute-start.21 = (bf16[128,1536]{1,0:T(8,128)(2,1)S(1)}, bf16[128,1536]{1,0:T(8,128)(2,1)S(1)}, u32[]{:S(2)}, u32[]{:S(2)}) collective-permute-start(bf16[128,1536]{1,0:T(8,128)(2,1)S(1)} %get-tuple-element.46), channel_id=1, source_target_pairs={{0,2},{1,3},{2,0},{3,1},{4,6},{5,7},{6,4},{7,5},{8,10},{9,11},{10,... | collective-permute-start | bytes 1179656 | tf_op jit(solution)/shard_map/ppermute | solution.py:28
  148.4 11.5 %collective-permute-start.23 = (bf16[128,1536]{1,0:T(8,128)(2,1)S(1)}, bf16[128,1536]{1,0:T(8,128)(2,1)S(1)}, u32[]{:S(2)}, u32[]{:S(2)}) collective-permute-start(bf16[128,1536]{1,0:T(8,128)(2,1)S(1)} %get-tuple-element.47), channel_id=1, source_target_pairs={{0,4},{1,5},{2,6},{3,7},{4,0},{5,1},{6,2},{7,3},{8,12},{9,13},{10,... | collective-permute-start | bytes 1179656 | tf_op jit(solution)/shard_map/ppermute | solution.py:24
  217.7 13.7 %collective-permute-start.33 = (bf16[528,384]{1,0:T(8,128)(2,1)S(1)}, bf16[528,384]{1,0:T(8,128)(2,1)S(1)}, u32[]{:S(2)}, u32[]{:S(2)}) collective-permute-start(bf16[528,384]{1,0:T(8,128)(2,1)S(1)} %get-tuple-element.39), channel_id=1, source_target_pairs={{0,16},{8,24},{16,32},{24,40},{32,48},{40,56},{48,0},{56,8},{64,80... | collective-permute-start | bytes 1216520 | tf_op jit(solution)/shard_map/ppermute | solution.py:463
  232.2 29.2 %collective-permute-start.34 = (bf16[4,528,256]{2,1,0:T(8,128)(2,1)S(1)}, bf16[4,528,256]{2,1,0:T(8,128)(2,1)}, u32[]{:S(2)}, u32[]{:S(2)}) collective-permute-start(bf16[4,528,256]{2,1,0:T(8,128)(2,1)S(1)} %pad_maximum_fusion.2.kv), channel_id=1, source_target_pairs={{0,64},{8,72},{16,80},{24,88},{32,96},{40,104},{48,112},{56,120},{... | collective-permute-start | bytes 3244040 | tf_op jit(solution)/shard_map/ppermute | solution.py:585
  262.3 23.9 %collective-permute-start.37 = (bf16[256,1536]{1,0:T(8,128)(2,1)S(1)}, bf16[256,1536]{1,0:T(8,128)(2,1)S(1)}, u32[]{:S(2)}, u32[]{:S(2)}) collective-permute-start(bf16[256,1536]{1,0:T(8,128)(2,1)S(1)} %get-tuple-element.43), channel_id=1, source_target_pairs={{0,2},{1,3},{2,0},{3,1},{4,6},{5,7},{6,4},{7,5},{8,10},{9,11},{10,... | collective-permute-start | bytes 2359304 | tf_op jit(solution)/shard_map/ppermute | solution.py:28
  262.4 23.8 %collective-permute-start.39 = (bf16[256,1536]{1,0:T(8,128)(2,1)S(1)}, bf16[256,1536]{1,0:T(8,128)(2,1)S(1)}, u32[]{:S(2)}, u32[]{:S(2)}) collective-permute-start(bf16[256,1536]{1,0:T(8,128)(2,1)S(1)} %get-tuple-element.44), channel_id=1, source_target_pairs={{0,4},{1,5},{2,6},{3,7},{4,0},{5,1},{6,2},{7,3},{8,12},{9,13},{10,... | collective-permute-start | bytes 2359304 | tf_op jit(solution)/shard_map/ppermute | solution.py:24
  286.5 13.1 %collective-permute-start.38 = (bf16[128,1536]{1,0:T(8,128)(2,1)S(1)}, bf16[128,1536]{1,0:T(8,128)(2,1)S(1)}, u32[]{:S(2)}, u32[]{:S(2)}) collective-permute-start(bf16[128,1536]{1,0:T(8,128)(2,1)S(1)} %get-tuple-element.42), channel_id=1, source_target_pairs={{0,4},{1,5},{2,6},{3,7},{4,0},{5,1},{6,2},{7,3},{8,12},{9,13},{10,... | collective-permute-start | bytes 1179656 | tf_op jit(solution)/shard_map/ppermute | solution.py:24
  288.5 34.0 %collective-permute-start.40 = (bf16[128,1536]{1,0:T(8,128)(2,1)S(1)}, bf16[128,1536]{1,0:T(8,128)(2,1)S(1)}, u32[]{:S(2)}, u32[]{:S(2)}) collective-permute-start(bf16[128,1536]{1,0:T(8,128)(2,1)S(1)} %get-tuple-element.30), channel_id=1, source_target_pairs={{0,1},{1,2},{2,3},{3,0},{4,5},{5,6},{6,7},{7,4},{8,9},{9,10},{10,1... | collective-permute-start | bytes 1179656 | tf_op jit(solution)/shard_map/ppermute | solution.py:28
  289.2 33.3 %collective-permute-start.41 = (bf16[128,1536]{1,0:T(8,128)(2,1)S(1)}, bf16[128,1536]{1,0:T(8,128)(2,1)S(1)}, u32[]{:S(2)}, u32[]{:S(2)}) collective-permute-start(bf16[128,1536]{1,0:T(8,128)(2,1)S(1)} %get-tuple-element.31), channel_id=1, source_target_pairs={{0,3},{1,0},{2,1},{3,2},{4,7},{5,4},{6,5},{7,6},{8,11},{9,8},{10,9... | collective-permute-start | bytes 1179656 | tf_op jit(solution)/shard_map/ppermute | solution.py:28
  295.0 31.9 %collective-permute-start.45 = (bf16[1024,512]{1,0:T(8,128)(2,1)S(1)}, bf16[1024,512]{1,0:T(8,128)(2,1)S(1)}, u32[]{:S(2)}, u32[]{:S(2)}) collective-permute-start(bf16[1024,512]{1,0:T(8,128)(2,1)S(1)} %output_columns.4), channel_id=1, source_target_pairs={{0,2},{1,3},{2,0},{3,1},{4,6},{5,7},{6,4},{7,5},{8,10},{9,11},{10,... | collective-permute-start | bytes 3145736 | tf_op jit(solution)/shard_map/ppermute | solution.py:28
  299.2 27.6 %collective-permute-start.47 = (bf16[1024,512]{1,0:T(8,128)(2,1)S(1)}, bf16[1024,512]{1,0:T(8,128)(2,1)S(1)}, u32[]{:S(2)}, u32[]{:S(2)}) collective-permute-start(bf16[1024,512]{1,0:T(8,128)(2,1)S(1)} %output_columns.5), channel_id=1, source_target_pairs={{0,4},{1,5},{2,6},{3,7},{4,0},{5,1},{6,2},{7,3},{8,12},{9,13},{10,... | collective-permute-start | bytes 3145736 | tf_op jit(solution)/shard_map/ppermute | solution.py:24
  327.5 11.2 %collective-permute-start.48 = (bf16[512,512]{1,0:T(8,128)(2,1)S(1)}, bf16[512,512]{1,0:T(8,128)(2,1)S(1)}, u32[]{:S(2)}, u32[]{:S(2)}) collective-permute-start(bf16[512,512]{1,0:T(8,128)(2,1)S(1)} %get-tuple-element.26), channel_id=1, source_target_pairs={{0,1},{1,2},{2,3},{3,0},{4,5},{5,6},{6,7},{7,4},{8,9},{9,10},{10,1... | collective-permute-start | bytes 1572872 | tf_op jit(solution)/shard_map/ppermute | solution.py:28
  (49 other events, 379.1 us)
Sparse Core Ops, SparseCore 0:
  71.2 65.1 all-gather.2
